TPU v7x, 256 devices: a whole 4x4x8 slice. The times are simulated.
256 devices in a mesh: dp: 32 (over z, y_hi, core), tensor: 8 (over y_lo, x).
Axes of the slice: x: 4, y: 4 (y_hi: 2, y_lo: 2; y = y_hi * 2 + y_lo), z: 8, core: 2. Of those that a mesh axis runs over, the one named last changes fastest.
Arguments:
- x_ckpt: bfloat16 [10240, 5120], P('dp', 'tensor'), may hold values from -6 to 6
- norm_gain_vector: float32 [5120], replicated, may hold values from 0.25 to 1.75
- w_qkv: bfloat16 [5120, 3, 3072], P(None, None, 'tensor'), may hold values from -4 to 4
- segments: int32 [10240], P('dp'), may hold values from 0 to 212, never falling along the last dimension, each value on 1 to 96 neighbouring positions
- d_context: bfloat16 [10240, 3072], P('dp', 'tensor'), may hold values from -6 to 6
Outputs:
- input_gradient: bfloat16 [10240, 5120], P('dp', 'tensor')
- gain_gradient: float32 [5120], P('tensor')
- d_weight: bfloat16 [5120, 3, 3072], P('dp', None, 'tensor')
Inputs may be any that keep to these rules, and one draw needn't show every extreme that they name: `segments`: segment numbers never fall along the tokens.
All inputs are finite; a program needn't handle non-finite values.
Results may differ from a plain program's by a relative error of at most 0.022.
Values may be sent and summed in bfloat16 or wider, within the bound.
No kernel may reach another device: no remote copies, remote signals or barrier semaphores. Data moves between devices by JAX's collectives and lax.ppermute only.
A program may use at most 192 MiB of HBM per device.

v0:
```python
import jax
import jax.numpy as jnp
from jax import lax
from jax.sharding import PartitionSpec as P

HD = 128


def rotate(values, cosines, sines):
    half_size = values.shape[-1] // 2
    first = values[..., :half_size]
    second = values[..., half_size:]
    return jnp.concatenate(
        [first * cosines - second * sines, second * cosines + first * sines], axis=-1
    )


def rope_tables(length, head_size):
    half_size = head_size // 2
    positions = jnp.arange(length, dtype=jnp.float32)[:, None, None]
    inv_freq = 10000.0 ** (-(2.0 * jnp.arange(half_size, dtype=jnp.float32)) / head_size)
    angles = positions * inv_freq[None, None, :]
    return (jnp.cos(angles), jnp.sin(angles))


def attend(queries, key_rows, values, allowed, cosines, sines):
    rotated_q = rotate(queries, cosines, sines)
    rotated_k = rotate(key_rows, cosines, sines)
    scale = queries.shape[-1] ** (-0.5)
    scores = (
        jnp.einsum("qhd,khd->hqk", rotated_q, rotated_k, precision=lax.Precision.HIGHEST) * scale
    )
    scores = jnp.where(allowed[None], scores, -1e30)
    weights = jax.nn.softmax(scores, axis=-1)
    return jnp.einsum("hqk,khd->qhd", weights, values, precision=lax.Precision.HIGHEST)


def body(x_ckpt, norm_gain_vector, w_qkv, segments, d_context):
    local_width_share = x_ckpt.shape[1]
    whole = lax.all_gather(x_ckpt, "tensor", axis=1, tiled=True)
    input_rows = whole.astype(jnp.float32)
    row_inverse_scale = jnp.sqrt(jnp.mean(input_rows * input_rows, axis=1, keepdims=True) + 1e-05)
    unit_rows = input_rows / row_inverse_scale
    normalized_rows = (unit_rows * norm_gain_vector).astype(jnp.bfloat16)
    model_width, qkv_count, local_cols = w_qkv.shape
    weight_flat = w_qkv.reshape(model_width, qkv_count * local_cols)
    packed = jnp.dot(normalized_rows, weight_flat, preferred_element_type=jnp.float32).astype(
        jnp.bfloat16
    )
    length = normalized_rows.shape[0]
    heads_local = local_cols // HD
    heads_data = packed.astype(jnp.float32).reshape(length, qkv_count, heads_local, HD)
    row_ids = jnp.arange(length, dtype=jnp.int32)
    allowed = (segments[:, None] == segments[None, :]) & (row_ids[None, :] <= row_ids[:, None])
    cosines, sines = rope_tables(length, HD)

    def attend_local(queries, key_rows, values):
        return attend(queries, key_rows, values, allowed, cosines, sines)

    _, pullback = jax.vjp(attend_local, heads_data[:, 0], heads_data[:, 1], heads_data[:, 2])
    pulled = pullback(d_context.astype(jnp.float32).reshape(length, heads_local, HD))
    d_packed = (
        jnp.stack(pulled, axis=1).reshape(length, qkv_count * local_cols).astype(jnp.bfloat16)
    )
    partial_in = lax.dot_general(
        d_packed, weight_flat, (((1,), (1,)), ((), ())), preferred_element_type=jnp.float32
    )
    leading_column = lax.axis_index("tensor") * local_width_share
    unit_rows_owned = lax.dynamic_slice_in_dim(unit_rows, leading_column, local_width_share, 1)
    gain_owned_slice = lax.dynamic_slice_in_dim(
        norm_gain_vector, leading_column, local_width_share, 0
    )
    reduced_total = lax.psum(partial_in.astype(jnp.bfloat16), "tensor").astype(jnp.float32)
    blended_products = jnp.mean(reduced_total * norm_gain_vector * unit_rows, axis=1, keepdims=True)
    normalized_gradient = lax.dynamic_slice_in_dim(
        reduced_total, leading_column, local_width_share, 1
    )
    input_gradient = (
        (normalized_gradient * gain_owned_slice - unit_rows_owned * blended_products)
        / row_inverse_scale
    ).astype(jnp.bfloat16)
    gain_gradient = lax.psum(jnp.sum(normalized_gradient * unit_rows_owned, axis=0), "dp")
    rows_owned = model_width // lax.axis_size("dp")
    d_weight = lax.psum_scatter(
        lax.dot_general(
            normalized_rows, d_packed, (((0,), (0,)), ((), ())), preferred_element_type=jnp.float32
        ).astype(jnp.bfloat16),
        "dp",
        scatter_dimension=0,
        tiled=True,
    ).astype(jnp.float32)
    d_weight = d_weight.reshape(rows_owned, qkv_count, local_cols).astype(jnp.bfloat16)
    return (input_gradient, gain_gradient, d_weight)


def solution(mesh):
    in_specs = (P("dp", "tensor"), P(), P(None, None, "tensor"), P("dp"), P("dp", "tensor"))
    out_specs = (P("dp", "tensor"), P("tensor"), P("dp", None, "tensor"))
    return jax.shard_map(body, mesh=mesh, in_specs=in_specs, out_specs=out_specs, check_vma=False)
```

profile of v0, /device:TPU:2, one launch (start us, length us, event | category | flops | bytes accessed | tf_op | source)
XLA Modules:
  0.0 383.5 jit_solution(3650384821187119794)
XLA Ops:
  7.2 0.0 all-gather.2.cloned.1.call-start
  7.2 0.7 all-gather.2.cloned.1.call-update
  7.9 0.0 copy-start.5
  7.9 0.0 copy-start.7
  7.9 0.0 all-reduce.6.cloned.1.call-start
  8.0 15.4 %copy.13 = bf16[5120,3,384]{0,2,1:T(8,128)(2,1)} copy(bf16[5120,3,384]{2,0,1:T(8,128)(2,1)} %param.7) | data formatting | bytes 23592960 | tf_op args[2]
  23.3 0.0 copy-done.5
  23.4 0.9 copy.16
  24.3 0.0 copy-done.7
  24.3 0.8 fusion.12
  25.0 0.0 copy-start.6
  25.0 1.3 fusion.15
  26.3 32.4 %all-gather.2.cloned.1.call-done = bf16[320,5120]{1,0:T(8,128)(2,1)} async-done(((bf16[320,640]{1,0:T(8,128)(2,1)}), bf16[320,5120]{1,0:T(8,128)(2,1)}) %all-gather.2.cloned.1.call-update) | async-done | bytes 3276816 | tf_op jit(solution)/shard_map/all_gather | solution.py:40
  58.7 0.0 copy-start
  58.7 2.8 fusion
  61.6 0.0 copy-done.6
  61.6 0.1 copy-done
  61.6 8.3 %convolution_convert_fusion.2 = bf16[320,1152]{1,0:T(8,128)(2,1)} fusion(bf16[5120,1152]{0,1:T(8,128)(2,1)} %bitcast.49, f32[5120]{0:T(1024)S(1)} %copy-done.6, bf16[320,5120]{1,0:T(8,128)(2,1)S(1)} %copy-done, f32[320]{0:T(512)S(1)} %add_sqrt_fusion), kind=kOutput, calls=%fused_computation.7 | convolution fusion | flops 3781795840 | bytes 15832320 | tf_op jit(solution)/shard_map/dot_general | solution.py:47
  70.0 2.2 copy.14
  72.2 2.3 copy.15
  74.4 1.2 reshape.147
  75.7 0.0 copy-start.2
  75.7 0.1 slice_bitcast_fusion.1
  75.8 0.8 copy-done.2
  76.6 0.0 copy-start.4
  76.6 0.5 multiply_subtract_fusion.1
  77.1 0.4 copy-done.4
  77.5 1.6 fusion.21
  79.1 0.0 copy-start.3
  79.1 0.2 fusion.9
  79.3 0.7 copy-done.3
  80.1 1.4 fusion.3
  81.5 2.1 convolution_bitcast_fusion
  83.6 3.3 convolution_bitcast_fusion.1
  86.9 1.0 fusion.6
  87.9 0.4 multiply_add_fusion.3
  88.3 0.3 add_bitcast_fusion
  88.7 1.0 maximum_convert_fusion
  89.6 2.2 copy.21
  91.9 10.9 %convolution_convert_fusion.1 = bf16[320,5120]{1,0:T(8,128)(2,1)} fusion(bf16[320,1152]{0,1:T(8,128)(2,1)} %bitcast.54, bf16[5120,1152]{0,1:T(8,128)(2,1)} %bitcast.50), kind=kOutput, calls=%fused_computation.3 | convolution fusion | flops 3776512000 | bytes 15810560 | tf_op jit(solution)/shard_map/dot_general | solution.py:65
  102.8 0.0 all-reduce.6.cloned.1.call-update
  102.8 0.0 reduce-scatter.2.cloned.1.call-start
  102.9 11.0 %convolution_convert_fusion = bf16[5120,1152]{1,0:T(8,128)(2,1)} fusion(bf16[320,1152]{0,1:T(8,128)(2,1)} %bitcast.55, f32[5120]{0:T(1024)S(1)} %copy-done.6, bf16[320,5120]{1,0:T(8,128)(2,1)S(1)} %copy-done, f32[320]{0:T(512)S(1)} %add_sqrt_fusion), kind=kOutput, calls=%fused_computation | convolution fusion | flops 3787325440 | bytes 15832320 | tf_op jit(solution)/shard_map/dot_general | solution.py:85
  113.8 0.0 reduce-scatter.2.cloned.1.call-update
  113.9 0.1 dynamic_slice.10
  114.0 85.4 %all-reduce.6.cloned.1.call-done = bf16[320,5120]{1,0:T(8,128)(2,1)} async-done(((bf16[320,5120]{1,0:T(8,128)(2,1)}), bf16[320,5120]{1,0:T(8,128)(2,1)}) %all-reduce.6.cloned.1.call-update) | async-done | bytes 3276816 | tf_op jit(solution)/shard_map/psum | solution.py:73
  199.4 0.0 copy-start.1
  199.4 2.8 convert_element_type.47
  202.2 0.1 copy-done.1
  202.3 2.2 multiply_reduce_fusion
  204.5 1.0 multiply_reduce_fusion.1
  205.5 69.4 %psum.15 = f32[640]{0:T(1024)} all-reduce(f32[640]{0:T(1024)S(1)} %get-tuple-element.9), channel_id=1, replica_groups=mesh['dp'=32,'tensor'=8] {'dp'}, use_global_device_ids=true, to_apply=%region_7.8 | all-reduce | flops 640 | bytes 5120 | tf_op jit(solution)/shard_map/psum | solution.py:82
  274.9 100.2 %reduce-scatter.2.cloned.1.call-done = bf16[160,1152]{1,0:T(8,128)(2,1)} async-done(((bf16[5120,1152]{1,0:T(8,128)(2,1)}), bf16[160,1152]{1,0:T(8,128)(2,1)}) %reduce-scatter.2.cloned.1.call-update) | async-done | bytes 368656 | tf_op jit(solution)/shard_map/reduce_scatter | solution.py:84
  375.2 1.8 copy.28
  (5 shorter events, 0.0 us)
Async XLA Ops:
  7.2 51.6 %all-gather.2.cloned.1.call-start = ((), (), s32[]{:S(2)}) async-start(), calls=%async_computation.1 | async-start | bytes 3686400 | tf_op jit(solution)/shard_map/all_gather | solution.py:40
  7.9 15.5 %copy-start.5 = (bf16[320,384]{1,0:T(8,128)(2,1)S(1)}, bf16[320,384]{1,0:T(8,128)(2,1)}, u32[]{:S(2)}) copy-start(bf16[320,384]{1,0:T(8,128)(2,1)} %param.9) | copy-start | bytes 737284
  7.9 16.4 %copy-start.7 = (s32[320]{0:T(512)S(1)}, s32[320]{0:T(512)}, u32[]{:S(2)}) copy-start(s32[320]{0:T(512)} %param.8) | copy-start | bytes 3844
  7.9 191.4 %all-reduce.6.cloned.1.call-start = ((), (), s32[]{:S(2)}) async-start(), calls=%async_computation.2 | async-start | bytes 6553600 | tf_op jit(solution)/shard_map/psum | solution.py:73
  25.0 36.5 %copy-start.6 = (f32[5120]{0:T(1024)S(1)}, f32[5120]{0:T(1024)}, u32[]{:S(2)}) copy-start(f32[5120]{0:T(1024)} %param.6) | copy-start | bytes 61444
  58.7 2.9 copy-start
  75.7 0.9 copy-start.2
  76.6 0.9 copy-start.4
  79.1 1.0 copy-start.3
  102.8 272.3 %reduce-scatter.2.cloned.1.call-start = ((), (), s32[]{:S(2)}) async-start(), calls=%async_computation.3 | async-start | bytes 12165120 | tf_op jit(solution)/shard_map/reduce_scatter | solution.py:84
  199.4 2.9 copy-start.1
Sparse Core Ops, SparseCore 0:
  9.8 48.8 all-gather.1
  102.9 96.3 all-reduce.5
  204.5 170.5 reduce-scatter.1
where the time goes:
time: 384 us; the launch traced here: 383 us
  waiting for transfers between devices  219 us (57%)
  blocking collectives  69.4 us (18%)
  matrix products  39.7 us (10%)
  local copies, waits for them, and re-layouts  27 us (7%)
  other arithmetic  14.6 us (4%)
  between operations  13.9 us (4%)
    reduce_scatter x1, waiting for transfers between devices, body(): lax.psum_scatter(lax.dot_general(normalized_rows, d_packed, (((0,), (0,))...  100 us
    psum x1, waiting for transfers between devices, body(): lax.psum(partial_in.astype(jnp.bfloat16), 'tensor').astype(jnp.float32)  85.4 us
    psum x1, blocking collectives, body(): lax.psum(jnp.sum(normalized_gradient * unit_rows_owned, axis=0), 'dp')  69.4 us
    all_gather x1, waiting for transfers between devices, body(): whole = lax.all_gather(x_ckpt, 'tensor', axis=1, tiled=True)  32.4 us
    unnamed x18, local copies, waits for them, and re-layouts  18.4 us
    dot_general x1, matrix products, body(): lax.dot_general(normalized_rows, d_packed, (((0,), (0,)), ((), ())), pref...  11 us
    dot_general x1, matrix products, body(): lax.dot_general(d_packed, weight_flat, (((1,), (1,)), ((), ())), preferre...  10.9 us
    dot_general x1, matrix products, body(): jnp.dot(normalized_rows, weight_flat, preferred_element_type=jnp.float32)  8.34 us
  transfers between devices with their start and end apart: 3, of which 3 were waited for; matrix products, arithmetic and copies ran while one was open for 9% of the time, Pallas kernels for 0%

commit v1 on v0

v1 whole, which is shorter than its diff:
```python
import jax
import jax.numpy as jnp
from jax import lax
from jax.experimental import pallas as pl
from jax.experimental.pallas import tpu as pltpu
from jax.sharding import Mesh, PartitionSpec as P

HD = 128
HEADS = 3
TOK = 320
D = 5120
COLS = 1152
SHARE = 640
PW = 256
QW = 384
BF = jnp.bfloat16
F32 = jnp.float32
VMEM_LIMIT = 44 * 1024 * 1024


def dot(a, b, dims):
    return lax.dot_general(a, b, (dims, ((), ())), preferred_element_type=F32)


NN = ((1,), (0,))
NT = ((1,), (1,))
TN = ((0,), (0,))


def cost(flops, nbytes):
    return pl.CostEstimate(flops=flops, bytes_accessed=nbytes, transcendentals=0)


def square_sum(values):
    width = values.shape[1]
    squares = values * values
    total = squares[:, :128]
    for start in range(128, width, 128):
        total = total + squares[:, start : start + 128]
    return total


def absorb(x, gain_ref, places, w_slot, sums):
    width = x.shape[1] // len(places)
    values = x.astype(F32)
    gains = jnp.concatenate([gain_ref[t] for t in places], axis=1)
    sums = square_sum(values) if sums is None else sums + square_sum(values)
    return dot((values * gains).astype(BF), w_slot, NN), sums


def project_first(place_ref, p_ref, q_ref, gp_ref, gq_ref, w_ref, acc_ref, sq_ref, wp, wq, sems):
    places_p = [place_ref[k] for k in range(4)]
    places_q = [place_ref[0], place_ref[4]]
    copies = []
    for i, t in enumerate(places_p):
        copies.append(
            pltpu.make_async_copy(w_ref.at[t, pl.ds(0, PW)], wp.at[pl.ds(i * PW, PW)], sems.at[i])
        )
    for i, t in enumerate(places_q):
        copies.append(
            pltpu.make_async_copy(
                w_ref.at[t, pl.ds(PW, QW)], wq.at[pl.ds(i * QW, QW)], sems.at[4 + i]
            )
        )
    for c in copies:
        c.start()
    for c in copies[:4]:
        c.wait()
    part, sums = absorb(p_ref[...], gp_ref, places_p, wp[...], None)
    acc_ref[...] = part
    for c in copies[4:]:
        c.wait()
    part, sums = absorb(q_ref[...], gq_ref, places_q, wq[...], sums)
    acc_ref[...] += part
    sq_ref[...] = sums


def split(values):
    high = values.astype(BF)
    return high, (values - high.astype(F32)).astype(BF)


def attention(
    place_ref, acc0_ref, sq0_ref, p_ref, q1_ref, q2_ref, q3_ref, gp_ref, gq_ref,
    cos_ref, sin_ref, seg_col_ref, seg_row_ref, dctx_ref, w_ref,
    dp_ref, stat_ref, acc, wp, wq, sems,
):
    places_p = [place_ref[4 + k] for k in range(4)]
    places_q = [[place_ref[k], place_ref[4 + k]] for k in range(1, 4)]
    copies_p, copies_q = [], []
    for i, t in enumerate(places_p):
        copies_p.append(
            pltpu.make_async_copy(w_ref.at[t, pl.ds(0, PW)], wp.at[pl.ds(i * PW, PW)], sems.at[i])
        )
    for g, pair in enumerate(places_q):
        for i, t in enumerate(pair):
            copies_q.append(
                pltpu.make_async_copy(
                    w_ref.at[t, pl.ds(PW, QW)],
                    wq.at[g, pl.ds(i * QW, QW)],
                    sems.at[4 + 2 * g + i],
                )
            )
    for c in copies_p + copies_q:
        c.start()
    sums = sq0_ref[...]
    for c in copies_p:
        c.wait()
    part, sums = absorb(p_ref[...], gp_ref, places_p, wp[...], sums)
    acc[...] = acc0_ref[...] + part
    for g, x_ref in enumerate((q1_ref, q2_ref, q3_ref)):
        copies_q[2 * g].wait()
        copies_q[2 * g + 1].wait()
        part, sums = absorb(x_ref[...], gq_ref, places_q[g], wq[g], sums)
        acc[...] += part
    mean_square = jnp.sum(sums, axis=1, keepdims=True) * (1.0 / D) + 1e-05
    inverse = lax.rsqrt(mean_square)
    cosines, sines = cos_ref[...], sin_ref[...]
    queries_at = lax.broadcasted_iota(jnp.int32, (TOK, TOK), 0)
    keys_at = lax.broadcasted_iota(jnp.int32, (TOK, TOK), 1)
    allowed = (seg_col_ref[...] == seg_row_ref[...]) & (keys_at <= queries_at)
    scale = HD ** (-0.5)
    row_dot = jnp.zeros((TOK, HD), F32)
    for h in range(HEADS):
        at = [slice(n * HEADS * HD + h * HD, n * HEADS * HD + (h + 1) * HD) for n in range(3)]
        raw = [acc[:, s] * inverse for s in at]
        q, k, v = (r.astype(BF) for r in raw)
        qf, kf = q.astype(F32), k.astype(F32)
        qr = qf * cosines + pltpu.roll(qf, HD // 2, 1) * sines
        kr = kf * cosines + pltpu.roll(kf, HD // 2, 1) * sines
        qh, ql = split(qr)
        kh, kl = split(kr)
        scores = (dot(qh, kh, NT) + (dot(qh, kl, NT) + dot(ql, kh, NT))) * scale
        scores = jnp.where(allowed, scores, -1e30)
        weights = jnp.exp(scores - jnp.max(scores, axis=1, keepdims=True))
        weights = weights / jnp.sum(weights, axis=1, keepdims=True)
        cotangent = dctx_ref[:, h * HD : (h + 1) * HD]
        d_weights = dot(cotangent, v, NT)
        d_scores = weights * (
            d_weights - jnp.sum(weights * d_weights, axis=1, keepdims=True)
        )
        d_scores = (d_scores * scale).astype(BF)
        dv = dot(weights.astype(BF), cotangent, TN)
        dqr = dot(d_scores, kh, NN)
        dkr = dot(d_scores, qh, TN)
        dq = dqr * cosines + pltpu.roll(dqr * sines, HD // 2, 1)
        dk = dkr * cosines + pltpu.roll(dkr * sines, HD // 2, 1)
        for s, r, g in zip(at, raw, (dq, dk, dv)):
            row_dot += r * g
            dp_ref[:, s] = (g * inverse).astype(BF)
    total = jnp.sum(row_dot, axis=1, keepdims=True) * (1.0 / D)
    lane = lax.broadcasted_iota(jnp.int32, (TOK, HD), 1)
    stat_ref[...] = jnp.where(lane == 0, total, inverse * inverse)


def feature_gradient(place_ref, dp_ref, w_ref, *rest):
    outs, (ws, sems, qs, ps, out_sems) = rest[:6], rest[6:]
    order = [(k, dy) for k in (2, 1, 3, 0) for dy in (1, 0)]
    copies = []
    for n, (k, dy) in enumerate(order):
        copies.append(
            pltpu.make_async_copy(w_ref.at[place_ref[dy * 4 + k]], ws.at[n], sems.at[n])
        )
    for c in copies:
        c.start()
    left = []
    dp = dp_ref[...]
    for n, (k, dy) in enumerate(order):
        copies[n].wait()
        out = dot(dp, ws[n], NT).astype(BF)
        ps[dy, :, k * PW : (k + 1) * PW] = out[:, :PW]
        qs[k, :, dy * QW : (dy + 1) * QW] = out[:, PW:]
        if dy == 0:
            c = pltpu.make_async_copy(qs.at[k], outs[k], out_sems.at[k])
            c.start()
            left.append(c)
    for dy in (1, 0):
        c = pltpu.make_async_copy(ps.at[dy], outs[4 + dy], out_sems.at[4 + dy])
        c.start()
        left.append(c)
    for c in left:
        c.wait()


def weight_gradient(x_ref, d0, d1, d2, d3, out_ref, rhs, sems):
    @pl.when(pl.program_id(0) == 0)
    def _():
        copies = [
            pltpu.make_async_copy(d, rhs.at[pl.ds(i * TOK, TOK)], sems.at[i])
            for i, d in enumerate((d0, d1, d2, d3))
        ]
        for c in copies:
            c.start()
        for c in copies:
            c.wait()

    out_ref[...] = dot(x_ref[...], rhs[...], NN).astype(BF)


VM = pl.BlockSpec(memory_space=pltpu.VMEM)
SM = pl.BlockSpec(memory_space=pltpu.SMEM)
ANY = pl.BlockSpec(memory_space=pl.ANY)
PARAMS = pltpu.CompilerParams(vmem_limit_bytes=VMEM_LIMIT)


def shift(values, axis, by, size):
    return lax.ppermute(values, axis, [(i, (i + by) % size) for i in range(size)])


def swap(values, axis, bit, size):
    return lax.ppermute(values, axis, [(i, i ^ bit) for i in range(size)])


def body(x_own, gain, w_qkv, segments, d_context):
    yh, core = lax.axis_index("yh"), lax.axis_index("core")
    yl, x_at = lax.axis_index("yl"), lax.axis_index("x")
    ks = jnp.arange(4, dtype=jnp.int32)
    rows = [yl, 1 - yl]
    sources = jnp.concatenate([r * 4 + (x_at - ks) % 4 for r in rows]).astype(jnp.int32)
    targets = jnp.concatenate([r * 4 + (x_at + ks) % 4 for r in rows]).astype(jnp.int32)
    gain_own = lax.dynamic_slice_in_dim(gain, (yl * 4 + x_at) * SHARE, SHARE, 0)

    xp, xq = x_own[:, :PW], x_own[:, PW:]
    got_p = [shift(xp, "x", k, 4) for k in (1, 2, 3)]
    got_q = swap(xq, "yl", 1, 2)
    p_here = jnp.concatenate([xp] + got_p, axis=1)
    q_here = jnp.concatenate([xq, got_q], axis=1)
    p_there = swap(p_here, "yl", 1, 2)
    q_there = [shift(q_here, "x", k, 4) for k in (1, 2, 3)]

    scaled = (x_own.astype(F32) * gain_own).astype(BF).T.reshape(2, 2, 160, TOK)
    to_core = lax.dynamic_index_in_dim(scaled, 1 - core, 1, False)
    mine = lax.dynamic_index_in_dim(scaled, core, 1, False)
    pair = jnp.stack([mine, swap(to_core, "core", 1, 2)], axis=2)
    kept = lax.dynamic_index_in_dim(pair, yh, 0, False)
    got = swap(lax.dynamic_index_in_dim(pair, 1 - yh, 0, False), "yh", 1, 2)
    quarter = jnp.concatenate([kept, got], axis=1).reshape(160, 4 * TOK)
    group_x = lax.all_gather(quarter, ("yl", "x"), axis=0, tiled=True)

    weight = w_qkv.reshape(8, SHARE, COLS)
    gains = gain.reshape(8, 1, SHARE)
    gain_p, gain_q = gains[:, :, :PW], gains[:, :, PW:]
    acc, squares = pl.pallas_call(
        project_first,
        out_shape=(
            jax.ShapeDtypeStruct((TOK, COLS), F32),
            jax.ShapeDtypeStruct((TOK, 128), F32),
        ),
        in_specs=[SM, VM, VM, VM, VM, ANY],
        out_specs=(VM, VM),
        scratch_shapes=[
            pltpu.VMEM((4 * PW, COLS), BF),
            pltpu.VMEM((2 * QW, COLS), BF),
            pltpu.SemaphoreType.DMA((6,)),
        ],
        compiler_params=PARAMS,
        cost_estimate=cost(2 * TOK * 1792 * COLS, 8_000_000),
        name="project_first",
    )(sources, p_here, q_here, gain_p, gain_q, weight)

    half = HD // 2
    angles = jnp.arange(TOK, dtype=F32)[:, None] * (
        10000.0 ** (-(2.0 * jnp.arange(half, dtype=F32)) / HD)
    )
    cosines, sines = jnp.cos(angles), jnp.sin(angles)
    cosines = jnp.concatenate([cosines, cosines], axis=1)
    sines = jnp.concatenate([-sines, sines], axis=1)
    d_packed, stats = pl.pallas_call(
        attention,
        out_shape=(
            jax.ShapeDtypeStruct((TOK, COLS), BF),
            jax.ShapeDtypeStruct((TOK, HD), F32),
        ),
        in_specs=[SM] + [VM] * 13 + [ANY],
        out_specs=(VM, VM),
        scratch_shapes=[
            pltpu.VMEM((TOK, COLS), F32),
            pltpu.VMEM((4 * PW, COLS), BF),
            pltpu.VMEM((3, 2 * QW, COLS), BF),
            pltpu.SemaphoreType.DMA((10,)),
        ],
        compiler_params=PARAMS,
        cost_estimate=cost(2 * TOK * 3328 * COLS + 4_000_000_000, 14_000_000),
        name="attention",
    )(
        sources, acc, squares, p_there, *q_there, gain_p, gain_q, cosines, sines,
        segments[:, None], segments[None, :], d_context, weight,
    )

    from_yh = swap(d_packed, "yh", 1, 2)
    from_core = swap(d_packed, "core", 1, 2)
    from_both = swap(from_yh, "core", 1, 2)

    wide, narrow = 2 * QW, 4 * PW
    pieces = pl.pallas_call(
        feature_gradient,
        out_shape=tuple(
            [jax.ShapeDtypeStruct((TOK, wide), BF)] * 4
            + [jax.ShapeDtypeStruct((TOK, narrow), BF)] * 2
        ),
        in_specs=[SM, VM, ANY],
        out_specs=(ANY,) * 6,
        scratch_shapes=[
            pltpu.VMEM((8, SHARE, COLS), BF),
            pltpu.SemaphoreType.DMA((8,)),
            pltpu.VMEM((4, TOK, wide), BF),
            pltpu.VMEM((2, TOK, narrow), BF),
            pltpu.SemaphoreType.DMA((6,)),
        ],
        compiler_params=PARAMS,
        cost_estimate=cost(2 * TOK * D * COLS, 16_000_000),
        name="feature_gradient",
    )(targets, d_packed, weight)
    along_x = [shift(pieces[k], "x", k, 4) for k in (1, 2, 3)]
    along_y = swap(pieces[5], "yl", 1, 2)
    row_dots = lax.all_gather(stats[:, 0], ("yl", "x"), axis=0)
    sum_q = sum((a.astype(F32) for a in along_x), pieces[0].astype(F32))
    sum_p = pieces[4].astype(F32) + along_y.astype(F32)
    sent_q = swap(sum_q[:, QW:].astype(BF), "yl", 1, 2)
    sent_p = [
        shift(sum_p[:, k * PW : (k + 1) * PW].astype(BF), "x", k, 4) for k in (1, 2, 3)
    ]
    own_q = sum_q[:, :QW] + sent_q.astype(F32)
    own_p = sum((a.astype(F32) for a in sent_p), sum_p[:, :PW])
    d_normed = jnp.concatenate([own_p, own_q], axis=1)
    features = x_own.astype(F32)
    row_dot = jnp.sum(row_dots, axis=0) * stats[:, 1]
    input_gradient = (d_normed * gain_own - features * row_dot[:, None]).astype(BF)
    gain_gradient = jnp.sum(d_normed * features, axis=0).reshape(5, 128)
    for axis, bit, size in (
        ("core", 1, 2), ("yh", 1, 2), ("z", 1, 8), ("z", 2, 8), ("z", 4, 8),
    ):
        gain_gradient = gain_gradient + swap(gain_gradient, axis, bit, size)

    partial_weight = pl.pallas_call(
        weight_gradient,
        grid=(4,),
        out_shape=jax.ShapeDtypeStruct((1280, COLS), BF),
        in_specs=[pl.BlockSpec((320, 4 * TOK), lambda i: (i, 0))] + [ANY] * 4,
        out_specs=pl.BlockSpec((320, COLS), lambda i: (i, 0)),
        scratch_shapes=[pltpu.VMEM((4 * TOK, COLS), BF), pltpu.SemaphoreType.DMA((4,))],
        compiler_params=PARAMS,
        cost_estimate=cost(2 * 1280 * 1280 * COLS, 10_000_000),
        name="weight_gradient",
    )(group_x, d_packed, from_core, from_yh, from_both)
    d_weight = lax.psum_scatter(partial_weight, "z", scatter_dimension=0, tiled=True)
    return (
        input_gradient,
        gain_gradient.reshape(SHARE),
        d_weight.reshape(160, 3, HEADS * HD),
    )


def solution(mesh):
    fine = Mesh(mesh.devices.reshape(8, 2, 2, 2, 4), ("z", "yh", "core", "yl", "x"))
    dp, tensor = ("z", "yh", "core"), ("yl", "x")
    in_specs = (P(dp, tensor), P(), P(None, None, tensor), P(dp), P(dp, tensor))
    out_specs = (P(dp, tensor), P(tensor), P(dp, None, tensor))
    return jax.shard_map(
        body, mesh=fine, in_specs=in_specs, out_specs=out_specs, check_vma=False
    )
```

time: 384 us -> 298 us (0.78)
  waiting for transfers between devices: 219 us -> 101 us
  starting transfers between devices: 0.12 us -> 43.3 us
  matrix products: 39.7 us -> 0 us
  Pallas kernels: 0 us -> 31.6 us
  local copies, waits for them, and re-layouts: 27 us -> 58.5 us
  blocking collectives: 69.4 us -> 41.4 us
  other arithmetic: 14.6 us -> 6.17 us
    psum x1 -> x0, waiting for transfers between devices: 85.4 us -> none  [body(): lax.psum(partial_in.astype(jnp.bfloat16), 'tensor').astype(jnp.float32)]
    reduce_scatter x1, waiting for transfers between devices: 100 us -> 29.2 us  [body(): lax.psum_scatter(partial_weight, 'z', scatter_dimension=0, tiled=True)]
    psum x1 -> x0, blocking collectives: 69.4 us -> none  [body(): lax.psum(jnp.sum(normalized_gradient * unit_rows_owned, axis=0), 'dp')]
    reshape x1 -> x4, local copies, waits for them, and re-layouts: 2.27 us -> 51 us  [the longest x2 48 us: body(): weight = w_qkv.reshape(8, SHARE, COLS)]
    ppermute x0 -> x26, waiting for transfers between devices: none -> 43.3 us  [the longest x14 35.5 us: swap(): return lax.ppermute(values, axis, [(i, i ^ bit) for i in range(size)])]
    ppermute x0 -> x26, starting transfers between devices: none -> 43.2 us  [the longest x14 24 us: swap(): return lax.ppermute(values, axis, [(i, i ^ bit) for i in range(size)])]
    unnamed x0 -> x1, blocking collectives: none -> 41.4 us
    dot_general x8 -> x0, matrix products: 39.7 us -> none  [the longest x1 11 us: body(): lax.dot_general(normalized_rows, d_packed, (((0,), (0,)), ((), ())), pref...]
  transfers between devices with their start and end apart: 3 -> 28, of which waited for: 3 -> 16; matrix products, arithmetic and copies ran while one was open for 9% -> 19% of each run, Pallas kernels for 0% -> 1%
where the time goes in v1:
time: 298 us; the launch traced here: 297 us
  waiting for transfers between devices  101 us (34%)
  local copies, waits for them, and re-layouts  58.5 us (20%)
  starting transfers between devices  43.3 us (15%)
  blocking collectives  41.4 us (14%)
  Pallas kernels  31.6 us (11%)
  between operations  15 us (5%)
  other arithmetic  6.17 us (2%)
    reshape x2, local copies, waits for them, and re-layouts, body(): weight = w_qkv.reshape(8, SHARE, COLS)  48 us
    unnamed x1, blocking collectives  41.4 us
    ppermute x14, waiting for transfers between devices, swap(): return lax.ppermute(values, axis, [(i, i ^ bit) for i in range(size)])  35.5 us
    reduce_scatter x1, waiting for transfers between devices, body(): lax.psum_scatter(partial_weight, 'z', scatter_dimension=0, tiled=True)  29.2 us
    all_gather x1, waiting for transfers between devices, body(): group_x = lax.all_gather(quarter, ('yl', 'x'), axis=0, tiled=True)  28.2 us
    ppermute x14, starting transfers between devices, swap(): return lax.ppermute(values, axis, [(i, i ^ bit) for i in range(size)])  24 us
    ppermute x12, starting transfers between devices, shift(): lax.ppermute(values, axis, [(i, (i + by) % size) for i in range(size)])  19.2 us
    pallas_call x1, Pallas kernels, body(): pl.pallas_call(feature_gradient, out_shape=tuple([jax.ShapeDtypeStruct((T...  11 us
  transfers between devices with their start and end apart: 28, of which 16 were waited for; matrix products, arithmetic and copies ran while one was open for 19% of the time, Pallas kernels for 1%

profile of v1, /device:TPU:2, one launch (start us, length us, event | category | flops | bytes accessed | tf_op | source)
XLA Modules:
  0.0 296.8 jit_solution(1803315212066269533)
XLA Ops:
  7.2 0.9 slice.40
  8.2 1.6 collective-permute-start
  9.7 2.8 collective-permute-start.1
  12.6 0.4 collective-permute-start.2
  13.0 1.0 slice.41
  14.0 1.7 collective-permute-start.3
  15.8 2.6 collective-permute-done.1
  18.4 1.3 collective-permute-done.2
  19.7 1.8 collective-permute-start.4
  21.5 1.4 collective-permute-start.5
  22.9 1.7 collective-permute-start.6
  24.6 1.4 collective-permute-start.7
  26.2 18.9 %copy.36 = bf16[5120,3,384]{2,1,0:T(4,128)(2,1)} copy(bf16[5120,3,384]{2,0,1:T(8,128)(2,1)} %param.7) | data formatting | bytes 23592960 | tf_op jit(solution)/shard_map/reshape | solution.py:240
  45.2 29.1 %reshape.51.w_ref = bf16[8,640,1152]{2,1,0:T(8,128)(2,1)} reshape(bf16[5120,3,384]{2,1,0:T(4,128)(2,1)} %copy.36) | data formatting | bytes 23592960 | tf_op jit(solution)/shard_map/reshape | solution.py:240
  74.3 0.6 fusion.14
  74.9 0.2 pad_maximum_fusion.4
  75.1 4.1 %project_first.1 = (f32[320,1152]{1,0:T(8,128)S(1)}, f32[320,128]{1,0:T(8,128)S(1)}) custom-call(s32[8]{0:T(128)S(1)} %pad_add_fusion.1.place_ref, bf16[320,1024]{1,0:T(8,128)(2,1)S(1)} %pad_maximum_fusion.1.p_ref, bf16[320,768]{1,0:T(8,128)(2,1)S(1)} %pad_maximum_fusion.2.q_ref, f32[8,1,256]{2,1,0:T(1,128)S(1)} %slice.52.gp_ref, ...), custom_call_target="tpu_custom_call" | custom-call | flops 1321205760 | bytes 8000000 | tf_op jit(solution)/shard_map/project_first/pallas_call | solution.py:243
  79.3 0.8 copy-done.1
  80.1 1.0 copy-done.2
  81.1 9.4 %attention.1 = (bf16[320,1152]{1,0:T(8,128)(2,1)S(1)}, f32[320,128]{1,0:T(8,128)S(1)}) custom-call(s32[8]{0:T(128)S(1)} %pad_add_fusion.1.place_ref, f32[320,1152]{1,0:T(8,128)S(1)} %get-tuple-element.13.acc0_ref, f32[320,128]{1,0:T(8,128)S(1)} %get-tuple-element.14.sq0_ref, bf16[320,1024]{1,0:T(8,128)(2,1)S(1)} %collective-permute-done.4.p_ref, ...), custom_call_target="tpu_custom_call" | custom-call | flops 6453667840 | bytes 14000000 | tf_op jit(solution)/shard_map/attention/pallas_call | solution.py:268
  90.5 11.0 %feature_gradient.1 = (bf16[320,768]{1,0:T(8,128)(2,1)S(1)}, bf16[320,768]{1,0:T(8,128)(2,1)}, bf16[320,768]{1,0:T(8,128)(2,1)}, bf16[320,768]{1,0:T(8,128)(2,1)...) custom-call(s32[8]{0:T(128)S(1)} %pad_add_fusion.place_ref, ...), custom_call_target="tpu_custom_call" | custom-call | flops 3774873600 | bytes 16000000 | tf_op jit(solution)/shard_map/feature_gradient/pallas_call | solution.py:295
  101.5 0.7 collective-permute-start.12
  102.2 3.0 %collective-permute-start.13 = (bf16[320,768]{1,0:T(8,128)(2,1)}, bf16[320,768]{1,0:T(8,128)(2,1)}, u32[]{:S(2)}, u32[]{:S(2)}) collective-permute-start(bf16[320,768]{1,0:T(8,128)(2,1)} %get-tuple-element.20), channel_id=1, source_target_pairs={{0,2},{1,3},{2,0},{3,1},{4,6},{5,7},{6,4},{7,5},{8,10},{9,11},{10,... | collective-permute-start | bytes 1474568 | tf_op jit(solution)/shard_map/ppermute | solution.py:207
  105.2 0.8 collective-permute-start.8
  106.1 0.6 dynamic-slice
  107.3 0.1 slice_reduce_fusion
  107.5 0.3 dynamic-update-slice
  107.7 41.4 %all-reduce = f32[2560]{0:T(1024)S(1)} all-reduce(f32[2560]{0:T(1024)S(1)} %dynamic-update-slice), channel_id=2, replica_groups=mesh['z'=8,'yh'=2,'core'=2,'yl'=2,'x'=4] {'yl','x'}, use_global_device_ids=true, to_apply=%add | all-reduce | flops 2560 | bytes 20480
  149.2 0.2 fusion.11
  149.5 1.6 convert_add_fusion.1
  151.1 0.6 collective-permute-start.15
  151.7 1.4 fusion.19
  153.1 3.2 %collective-permute-start.10 = (bf16[320,256]{1,0:T(8,128)(2,1)S(1)}, bf16[320,256]{1,0:T(8,128)(2,1)S(1)}, u32[]{:S(2)}, u32[]{:S(2)}) collective-permute-start(bf16[320,256]{1,0:T(8,128)(2,1)S(1)} %get-tuple-element.41), channel_id=1, source_target_pairs={{0,2},{1,3},{2,0},{3,1},{4,6},{5,7},{6,4},{7,5},{8,10},{9,11},{10,... | collective-permute-start | bytes 491528 | tf_op jit(solution)/shard_map/ppermute | solution.py:207
  156.3 1.5 collective-permute-start.11
  157.8 1.4 collective-permute-start.9
  159.3 0.7 collective-permute-done.10
  160.0 2.5 collective-permute-done.11
  162.5 0.7 collective-permute-done.9
  163.3 1.0 fusion.2
  164.3 0.3 copy.33
  164.7 1.5 collective-permute-done.21
  166.2 0.1 fusion.10
  166.3 3.3 %collective-permute-start.22 = (bf16[160,2,320]{2,0,1:T(8,128)(2,1)S(1)}, bf16[160,2,320]{2,0,1:T(8,128)(2,1)S(1)}, u32[]{:S(2)}, u32[]{:S(2)}) collective-permute-start(bf16[160,2,320]{2,0,1:T(8,128)(2,1)S(1)} %get-tuple-element.43), channel_id=1, source_target_pairs={{0,16},{16,0},{1,17},{17,1},{2,18},{18,2},{3,19},{19,3},{4,20},{20... | collective-permute-start | bytes 614408 | tf_op jit(solution)/shard_map/ppermute | solution.py:211
  169.6 6.3 %collective-permute-done.22 = bf16[160,2,320]{2,0,1:T(8,128)(2,1)S(1)} collective-permute-done((bf16[160,2,320]{2,0,1:T(8,128)(2,1)S(1)}, bf16[160,2,320]{2,0,1:T(8,128)(2,1)S(1)}, u32[]{:S(2)}, u32[]{:S(2)}) %collective-permute-start.22) | collective-permute-done | bytes 204832 | tf_op jit(solution)/shard_map/ppermute | solution.py:211
  176.0 0.3 copy.34
  176.3 1.1 reshape.42
  177.5 3.3 %collective-permute-start.24 = (bf16[320,1152]{1,0:T(8,128)(2,1)S(1)}, bf16[320,1152]{1,0:T(8,128)(2,1)S(1)}, u32[]{:S(2)}, u32[]{:S(2)}) collective-permute-start(bf16[320,1152]{1,0:T(8,128)(2,1)S(1)} %get-tuple-element.15.dp_ref.d0), channel_id=1, source_target_pairs={{0,16},{16,0},{1,17},{17,1},{2,18},{18,2},{3,19},{19,3},{4,20},{20... | collective-permute-start | bytes 2211848 | tf_op jit(solution)/shard_map/ppermute | solution.py:211
  180.7 16.0 %collective-permute-done.24.d2 = bf16[320,1152]{1,0:T(8,128)(2,1)S(1)} collective-permute-done((bf16[320,1152]{1,0:T(8,128)(2,1)S(1)}, bf16[320,1152]{1,0:T(8,128)(2,1)S(1)}, u32[]{:S(2)}, u32[]{:S(2)}) %collective-permute-start.24) | collective-permute-done | bytes 737312 | tf_op jit(solution)/shard_map/ppermute | solution.py:211
  196.8 2.2 collective-permute-done.25.d3
  199.0 28.2 %all-gather.3.cloned.1.call-done.x_ref = bf16[1280,1280]{1,0:T(8,128)(2,1)} async-done(((bf16[160,1280]{1,0:T(8,128)(2,1)}), bf16[1280,1280]{1,0:T(8,128)(2,1)}) %all-gather.3.cloned.1.call-update) | async-done | bytes 3276816 | tf_op jit(solution)/shard_map/all_gather | solution.py:238
  227.2 1.9 copy-done
  229.1 7.1 %weight_gradient.1 = bf16[1280,1152]{1,0:T(8,128)(2,1)} custom-call(bf16[1280,1280]{1,0:T(8,128)(2,1)S(1)} %copy-done, bf16[320,1152]{1,0:T(8,128)(2,1)S(1)} %get-tuple-element.15.dp_ref.d0, bf16[320,1152]{1,0:T(8,128)(2,1)S(1)} %collective-permute-done.23.d1, bf16[320,1152]{1,0:T(8,128)(2,1)S(1)} %collective-permute-done.24.d2, ...), custom_call_target="tpu_custom_call" | custom-call | flops 3774873600 | bytes 10000000 | tf_op jit(solution)/shard_map/weight_gradient/pallas_call | solution.py:335
  236.4 1.2 collective-permute-done.16
  237.5 2.7 collective-permute-start.17
  240.3 2.4 collective-permute-done.17
  242.7 1.6 collective-permute-start.18
  244.2 2.1 collective-permute-done.18
  246.3 2.5 collective-permute-start.19
  248.8 2.0 collective-permute-done.19
  250.8 5.7 %collective-permute-start.20 = (f32[5,128]{1,0:T(8,128)S(1)}, f32[5,128]{1,0:T(8,128)S(1)}, u32[]{:S(2)}, u32[]{:S(2)}) collective-permute-start(f32[5,128]{1,0:T(8,128)S(1)} %add.128), channel_id=1, source_target_pairs={{0,128},{32,160},{64,192},{96,224},{128,0},{160,32},{192,64},{224,... | collective-permute-start | bytes 7688 | tf_op jit(solution)/shard_map/ppermute | solution.py:211
  256.5 1.9 collective-permute-done.20
  258.4 0.6 add_bitcast_fusion
  259.0 29.2 %reduce-scatter.2.cloned.1.call-done = bf16[160,1152]{1,0:T(8,128)(2,1)} async-done(((bf16[1280,1152]{1,0:T(8,128)(2,1)}), bf16[160,1152]{1,0:T(8,128)(2,1)}) %reduce-scatter.2.cloned.1.call-update) | async-done | bytes 368656 | tf_op jit(solution)/shard_map/reduce_scatter | solution.py:346
  288.2 1.8 copy.40
  (59 shorter events, 1.3 us)
Async XLA Ops:
  7.2 220.0 %all-gather.3.cloned.1.call-start = ((), (), s32[]{:S(2)}) async-start(), calls=%async_computation.1 | async-start | bytes 3686400 | tf_op jit(solution)/shard_map/all_gather | solution.py:238
  8.1 18.0 %copy-start.5 = (f32[5120]{0:T(1024)S(1)}, f32[5120]{0:T(1024)}, u32[]{:S(2)}) copy-start(f32[5120]{0:T(1024)} %param.6) | copy-start | bytes 61444
  8.2 18.0 %copy-start.6 = (s32[320]{0:T(512)S(1)}, s32[320]{0:T(512)}, u32[]{:S(2)}) copy-start(s32[320]{0:T(512)} %param.8) | copy-start | bytes 3844
  8.2 7.6 %collective-permute-start = (bf16[320,256]{1,0:T(8,128)(2,1)S(1)}, bf16[320,256]{1,0:T(8,128)(2,1)S(1)}, u32[]{:S(2)}, u32[]{:S(2)}) collective-permute-start(bf16[320,256]{1,0:T(8,128)(2,1)S(1)} %slice.40), channel_id=1, source_target_pairs={{0,1},{1,2},{2,3},{3,0},{4,5},{5,6},{6,7},{7,4},{8,9},{9,10},{10,1... | collective-permute-start | bytes 491528 | tf_op jit(solution)/shard_map/ppermute | solution.py:207
  9.7 8.6 %collective-permute-start.1 = (bf16[320,256]{1,0:T(8,128)(2,1)S(1)}, bf16[320,256]{1,0:T(8,128)(2,1)S(1)}, u32[]{:S(2)}, u32[]{:S(2)}) collective-permute-start(bf16[320,256]{1,0:T(8,128)(2,1)S(1)} %slice.40), channel_id=1, source_target_pairs={{0,2},{1,3},{2,0},{3,1},{4,6},{5,7},{6,4},{7,5},{8,10},{9,11},{10,... | collective-permute-start | bytes 491528 | tf_op jit(solution)/shard_map/ppermute | solution.py:207
  12.6 7.1 %collective-permute-start.2 = (bf16[320,256]{1,0:T(8,128)(2,1)S(1)}, bf16[320,256]{1,0:T(8,128)(2,1)S(1)}, u32[]{:S(2)}, u32[]{:S(2)}) collective-permute-start(bf16[320,256]{1,0:T(8,128)(2,1)S(1)} %slice.40), channel_id=1, source_target_pairs={{0,3},{1,0},{2,1},{3,2},{4,7},{5,4},{6,5},{7,6},{8,11},{9,8},{10,9... | collective-permute-start | bytes 491528 | tf_op jit(solution)/shard_map/ppermute | solution.py:207
  14.0 7.5 %collective-permute-start.3 = (bf16[320,384]{1,0:T(8,128)(2,1)S(1)}, bf16[320,384]{1,0:T(8,128)(2,1)S(1)}, u32[]{:S(2)}, u32[]{:S(2)}) collective-permute-start(bf16[320,384]{1,0:T(8,128)(2,1)S(1)} %slice.41), channel_id=1, source_target_pairs={{0,4},{4,0},{1,5},{5,1},{2,6},{6,2},{3,7},{7,3},{8,12},{12,8},{9,1... | collective-permute-start | bytes 737288 | tf_op jit(solution)/shard_map/ppermute | solution.py:211
  19.7 60.3 %collective-permute-start.4 = (bf16[320,1024]{1,0:T(8,128)(2,1)S(1)}, bf16[320,1024]{1,0:T(8,128)(2,1)S(1)}, u32[]{:S(2)}, u32[]{:S(2)}) collective-permute-start(bf16[320,1024]{1,0:T(8,128)(2,1)S(1)} %pad_maximum_fusion.1.p_ref), channel_id=1, source_target_pairs={{0,4},{4,0},{1,5},{5,1},{2,6},{6,2},{3,7},{7,3},{8,12},{12,8},{9,1... | collective-permute-start | bytes 1966088 | tf_op jit(solution)/shard_map/ppermute | solution.py:211
  21.5 57.7 %collective-permute-start.5 = (bf16[320,768]{1,0:T(8,128)(2,1)S(1)}, bf16[320,768]{1,0:T(8,128)(2,1)S(1)}, u32[]{:S(2)}, u32[]{:S(2)}) collective-permute-start(bf16[320,768]{1,0:T(8,128)(2,1)S(1)} %pad_maximum_fusion.2.q_ref), channel_id=1, source_target_pairs={{0,1},{1,2},{2,3},{3,0},{4,5},{5,6},{6,7},{7,4},{8,9},{9,10},{10,1... | collective-permute-start | bytes 1474568 | tf_op jit(solution)/shard_map/ppermute | solution.py:207
  22.9 56.4 %collective-permute-start.6 = (bf16[320,768]{1,0:T(8,128)(2,1)S(1)}, bf16[320,768]{1,0:T(8,128)(2,1)S(1)}, u32[]{:S(2)}, u32[]{:S(2)}) collective-permute-start(bf16[320,768]{1,0:T(8,128)(2,1)S(1)} %pad_maximum_fusion.2.q_ref), channel_id=1, source_target_pairs={{0,2},{1,3},{2,0},{3,1},{4,6},{5,7},{6,4},{7,5},{8,10},{9,11},{10,... | collective-permute-start | bytes 1474568 | tf_op jit(solution)/shard_map/ppermute | solution.py:207
  24.6 55.4 %collective-permute-start.7 = (bf16[320,768]{1,0:T(8,128)(2,1)S(1)}, bf16[320,768]{1,0:T(8,128)(2,1)}, u32[]{:S(2)}, u32[]{:S(2)}) collective-permute-start(bf16[320,768]{1,0:T(8,128)(2,1)S(1)} %pad_maximum_fusion.2.q_ref), channel_id=1, source_target_pairs={{0,3},{1,0},{2,1},{3,2},{4,7},{5,4},{6,5},{7,6},{8,11},{9,8},{10,9... | collective-permute-start | bytes 1474568 | tf_op jit(solution)/shard_map/ppermute | solution.py:207
  75.1 5.0 %copy-start.3 = (bf16[320,384]{1,0:T(8,128)(2,1)S(1)}, bf16[320,384]{1,0:T(8,128)(2,1)}, u32[]{:S(2)}) copy-start(bf16[320,384]{1,0:T(8,128)(2,1)} %dctx_ref.1) | copy-start | bytes 737284
  79.3 0.8 copy-start.1
  80.0 1.0 copy-start.2
  90.5 15.6 %copy-start.7 = (u32[256]{0:T(256)S(1)}, u32[256]{0:T(256)}, u32[]{:S(2)}) copy-start(u32[256]{0:T(256)} %constant.75) | copy-start | bytes 3076
  101.5 48.0 %collective-permute-start.12 = (bf16[320,768]{1,0:T(8,128)(2,1)}, bf16[320,768]{1,0:T(8,128)(2,1)}, u32[]{:S(2)}, u32[]{:S(2)}) collective-permute-start(bf16[320,768]{1,0:T(8,128)(2,1)} %get-tuple-element.19), channel_id=1, source_target_pairs={{0,1},{1,2},{2,3},{3,0},{4,5},{5,6},{6,7},{7,4},{8,9},{9,10},{10,1... | collective-permute-start | bytes 1474568 | tf_op jit(solution)/shard_map/ppermute | solution.py:207
  102.2 47.3 %collective-permute-start.13 = (bf16[320,768]{1,0:T(8,128)(2,1)}, bf16[320,768]{1,0:T(8,128)(2,1)}, u32[]{:S(2)}, u32[]{:S(2)}) collective-permute-start(bf16[320,768]{1,0:T(8,128)(2,1)} %get-tuple-element.20), channel_id=1, source_target_pairs={{0,2},{1,3},{2,0},{3,1},{4,6},{5,7},{6,4},{7,5},{8,10},{9,11},{10,... | collective-permute-start | bytes 1474568 | tf_op jit(solution)/shard_map/ppermute | solution.py:207
  105.2 44.3 %collective-permute-start.14 = (bf16[320,768]{1,0:T(8,128)(2,1)S(1)}, bf16[320,768]{1,0:T(8,128)(2,1)}, u32[]{:S(2)}, u32[]{:S(2)}) collective-permute-start(bf16[320,768]{1,0:T(8,128)(2,1)S(1)} %get-tuple-element.21), channel_id=1, source_target_pairs={{0,3},{1,0},{2,1},{3,2},{4,7},{5,4},{6,5},{7,6},{8,11},{9,8},{10,9... | collective-permute-start | bytes 1474568 | tf_op jit(solution)/shard_map/ppermute | solution.py:207
  105.2 46.5 %collective-permute-start.8 = (bf16[320,1024]{1,0:T(8,128)(2,1)S(1)}, bf16[320,1024]{1,0:T(8,128)(2,1)}, u32[]{:S(2)}, u32[]{:S(2)}) collective-permute-start(bf16[320,1024]{1,0:T(8,128)(2,1)S(1)} %get-tuple-element.17), channel_id=1, source_target_pairs={{0,4},{4,0},{1,5},{5,1},{2,6},{6,2},{3,7},{7,3},{8,12},{12,8},{9,1... | collective-permute-start | bytes 1966088 | tf_op jit(solution)/shard_map/ppermute | solution.py:211
  151.1 8.1 %collective-permute-start.15 = (bf16[320,384]{1,0:T(8,128)(2,1)S(1)}, bf16[320,384]{1,0:T(8,128)(2,1)S(1)}, u32[]{:S(2)}, u32[]{:S(2)}) collective-permute-start(bf16[320,384]{1,0:T(8,128)(2,1)S(1)} %slice.69), channel_id=1, source_target_pairs={{0,4},{4,0},{1,5},{5,1},{2,6},{6,2},{3,7},{7,3},{8,12},{12,8},{9,1... | collective-permute-start | bytes 737288 | tf_op jit(solution)/shard_map/ppermute | solution.py:211
  153.1 10.2 %copy-start.4 = (bf16[320,640]{1,0:T(8,128)(2,1)S(1)}, bf16[320,640]{1,0:T(8,128)(2,1)}, u32[]{:S(2)}) copy-start(bf16[320,640]{1,0:T(8,128)(2,1)} %param.5) | copy-start | bytes 1228804
  153.1 6.9 %collective-permute-start.10 = (bf16[320,256]{1,0:T(8,128)(2,1)S(1)}, bf16[320,256]{1,0:T(8,128)(2,1)S(1)}, u32[]{:S(2)}, u32[]{:S(2)}) collective-permute-start(bf16[320,256]{1,0:T(8,128)(2,1)S(1)} %get-tuple-element.41), channel_id=1, source_target_pairs={{0,2},{1,3},{2,0},{3,1},{4,6},{5,7},{6,4},{7,5},{8,10},{9,11},{10,... | collective-permute-start | bytes 491528 | tf_op jit(solution)/shard_map/ppermute | solution.py:207
  156.3 6.2 %collective-permute-start.11 = (bf16[320,256]{1,0:T(8,128)(2,1)S(1)}, bf16[320,256]{1,0:T(8,128)(2,1)S(1)}, u32[]{:S(2)}, u32[]{:S(2)}) collective-permute-start(bf16[320,256]{1,0:T(8,128)(2,1)S(1)} %get-tuple-element.40), channel_id=1, source_target_pairs={{0,3},{1,0},{2,1},{3,2},{4,7},{5,4},{6,5},{7,6},{8,11},{9,8},{10,9... | collective-permute-start | bytes 491528 | tf_op jit(solution)/shard_map/ppermute | solution.py:207
  157.8 5.3 %collective-permute-start.9 = (bf16[320,256]{1,0:T(8,128)(2,1)S(1)}, bf16[320,256]{1,0:T(8,128)(2,1)S(1)}, u32[]{:S(2)}, u32[]{:S(2)}) collective-permute-start(bf16[320,256]{1,0:T(8,128)(2,1)S(1)} %get-tuple-element.39), channel_id=1, source_target_pairs={{0,1},{1,2},{2,3},{3,0},{4,5},{5,6},{6,7},{7,4},{8,9},{9,10},{10,1... | collective-permute-start | bytes 491528 | tf_op jit(solution)/shard_map/ppermute | solution.py:207
  164.6 1.6 collective-permute-start.21
  166.3 9.6 %collective-permute-start.22 = (bf16[160,2,320]{2,0,1:T(8,128)(2,1)S(1)}, bf16[160,2,320]{2,0,1:T(8,128)(2,1)S(1)}, u32[]{:S(2)}, u32[]{:S(2)}) collective-permute-start(bf16[160,2,320]{2,0,1:T(8,128)(2,1)S(1)} %get-tuple-element.43), channel_id=1, source_target_pairs={{0,16},{16,0},{1,17},{17,1},{2,18},{18,2},{3,19},{19,3},{4,20},{20... | collective-permute-start | bytes 614408 | tf_op jit(solution)/shard_map/ppermute | solution.py:211
  177.4 110.7 %reduce-scatter.2.cloned.1.call-start = ((), (), s32[]{:S(2)}) async-start(), calls=%async_computation.2 | async-start | bytes 3317760 | tf_op jit(solution)/shard_map/reduce_scatter | solution.py:346
  177.5 19.3 %collective-permute-start.24 = (bf16[320,1152]{1,0:T(8,128)(2,1)S(1)}, bf16[320,1152]{1,0:T(8,128)(2,1)S(1)}, u32[]{:S(2)}, u32[]{:S(2)}) collective-permute-start(bf16[320,1152]{1,0:T(8,128)(2,1)S(1)} %get-tuple-element.15.dp_ref.d0), channel_id=1, source_target_pairs={{0,16},{16,0},{1,17},{17,1},{2,18},{18,2},{3,19},{19,3},{4,20},{20... | collective-permute-start | bytes 2211848 | tf_op jit(solution)/shard_map/ppermute | solution.py:211
  180.7 16.0 %collective-permute-start.23 = (bf16[320,1152]{1,0:T(8,128)(2,1)S(1)}, bf16[320,1152]{1,0:T(8,128)(2,1)S(1)}, u32[]{:S(2)}, u32[]{:S(2)}) collective-permute-start(bf16[320,1152]{1,0:T(8,128)(2,1)S(1)} %get-tuple-element.15.dp_ref.d0), channel_id=1, source_target_pairs={{0,8},{8,0},{1,9},{9,1},{2,10},{10,2},{3,11},{11,3},{4,12},{12,4},... | collective-permute-start | bytes 2211848 | tf_op jit(solution)/shard_map/ppermute | solution.py:211
  196.8 2.2 collective-permute-start.25
  227.2 1.9 copy-start
  236.3 1.3 collective-permute-start.16
  237.5 5.1 %collective-permute-start.17 = (f32[5,128]{1,0:T(8,128)S(1)}, f32[5,128]{1,0:T(8,128)S(1)}, u32[]{:S(2)}, u32[]{:S(2)}) collective-permute-start(f32[5,128]{1,0:T(8,128)S(1)} %bitcast_add_fusion), channel_id=1, source_target_pairs={{0,16},{16,0},{1,17},{17,1},{2,18},{18,2},{3,19},{19,3},{4,20},{20... | collective-permute-start | bytes 7688 | tf_op jit(solution)/shard_map/ppermute | solution.py:211
  242.7 3.6 %collective-permute-start.18 = (f32[5,128]{1,0:T(8,128)S(1)}, f32[5,128]{1,0:T(8,128)S(1)}, u32[]{:S(2)}, u32[]{:S(2)}) collective-permute-start(f32[5,128]{1,0:T(8,128)S(1)} %fusion.21), channel_id=1, source_target_pairs={{0,32},{32,0},{64,96},{96,64},{128,160},{160,128},{192,224},{224,1... | collective-permute-start | bytes 7688 | tf_op jit(solution)/shard_map/ppermute | solution.py:211
  246.3 4.5 %collective-permute-start.19 = (f32[5,128]{1,0:T(8,128)S(1)}, f32[5,128]{1,0:T(8,128)S(1)}, u32[]{:S(2)}, u32[]{:S(2)}) collective-permute-start(f32[5,128]{1,0:T(8,128)S(1)} %add.127), channel_id=1, source_target_pairs={{0,64},{32,96},{64,0},{96,32},{128,192},{160,224},{192,128},{224,1... | collective-permute-start | bytes 7688 | tf_op jit(solution)/shard_map/ppermute | solution.py:211
  250.8 7.6 %collective-permute-start.20 = (f32[5,128]{1,0:T(8,128)S(1)}, f32[5,128]{1,0:T(8,128)S(1)}, u32[]{:S(2)}, u32[]{:S(2)}) collective-permute-start(f32[5,128]{1,0:T(8,128)S(1)} %add.128), channel_id=1, source_target_pairs={{0,128},{32,160},{64,192},{96,224},{128,0},{160,32},{192,64},{224,... | collective-permute-start | bytes 7688 | tf_op jit(solution)/shard_map/ppermute | solution.py:211
Sparse Core Ops, SparseCore 0:
  177.5 49.6 all-gather.2
  236.4 51.7 reduce-scatter.1

commit v2 on v1

--- a/solution.py
+++ b/solution.py
@@ -48,27 +48,32 @@
     return dot((values * gains).astype(BF), w_slot, NN), sums
 
 
+def fetch(w_ref, place, first, count, slot, start, sems):
+    return [
+        pltpu.make_async_copy(
+            w_ref.at[n, pl.ds(place * SHARE + first, count)],
+            slot.at[pl.ds(start, count), pl.ds(n * HEADS * HD, HEADS * HD)],
+            sems.at[n],
+        )
+        for n in range(3)
+    ]
+
+
 def project_first(place_ref, p_ref, q_ref, gp_ref, gq_ref, w_ref, acc_ref, sq_ref, wp, wq, sems):
     places_p = [place_ref[k] for k in range(4)]
     places_q = [place_ref[0], place_ref[4]]
     copies = []
     for i, t in enumerate(places_p):
-        copies.append(
-            pltpu.make_async_copy(w_ref.at[t, pl.ds(0, PW)], wp.at[pl.ds(i * PW, PW)], sems.at[i])
-        )
+        copies += fetch(w_ref, t, 0, PW, wp, i * PW, sems.at[i])
     for i, t in enumerate(places_q):
-        copies.append(
-            pltpu.make_async_copy(
-                w_ref.at[t, pl.ds(PW, QW)], wq.at[pl.ds(i * QW, QW)], sems.at[4 + i]
-            )
-        )
+        copies += fetch(w_ref, t, PW, QW, wq, i * QW, sems.at[4 + i])
     for c in copies:
         c.start()
-    for c in copies[:4]:
+    for c in copies[:12]:
         c.wait()
     part, sums = absorb(p_ref[...], gp_ref, places_p, wp[...], None)
     acc_ref[...] = part
-    for c in copies[4:]:
+    for c in copies[12:]:
         c.wait()
     part, sums = absorb(q_ref[...], gq_ref, places_q, wq[...], sums)
     acc_ref[...] += part
@@ -89,18 +94,10 @@
     places_q = [[place_ref[k], place_ref[4 + k]] for k in range(1, 4)]
     copies_p, copies_q = [], []
     for i, t in enumerate(places_p):
-        copies_p.append(
-            pltpu.make_async_copy(w_ref.at[t, pl.ds(0, PW)], wp.at[pl.ds(i * PW, PW)], sems.at[i])
-        )
+        copies_p += fetch(w_ref, t, 0, PW, wp, i * PW, sems.at[i])
     for g, pair in enumerate(places_q):
         for i, t in enumerate(pair):
-            copies_q.append(
-                pltpu.make_async_copy(
-                    w_ref.at[t, pl.ds(PW, QW)],
-                    wq.at[g, pl.ds(i * QW, QW)],
-                    sems.at[4 + 2 * g + i],
-                )
-            )
+            copies_q += fetch(w_ref, t, PW, QW, wq.at[g], i * QW, sems.at[4 + 2 * g + i])
     for c in copies_p + copies_q:
         c.start()
     sums = sq0_ref[...]
@@ -109,8 +106,8 @@
     part, sums = absorb(p_ref[...], gp_ref, places_p, wp[...], sums)
     acc[...] = acc0_ref[...] + part
     for g, x_ref in enumerate((q1_ref, q2_ref, q3_ref)):
-        copies_q[2 * g].wait()
-        copies_q[2 * g + 1].wait()
+        for c in copies_q[6 * g : 6 * g + 6]:
+            c.wait()
         part, sums = absorb(x_ref[...], gq_ref, places_q[g], wq[g], sums)
         acc[...] += part
     mean_square = jnp.sum(sums, axis=1, keepdims=True) * (1.0 / D) + 1e-05
@@ -158,15 +155,15 @@
     order = [(k, dy) for k in (2, 1, 3, 0) for dy in (1, 0)]
     copies = []
     for n, (k, dy) in enumerate(order):
-        copies.append(
-            pltpu.make_async_copy(w_ref.at[place_ref[dy * 4 + k]], ws.at[n], sems.at[n])
-        )
-    for c in copies:
-        c.start()
+        copies.append(fetch(w_ref, place_ref[dy * 4 + k], 0, SHARE, ws.at[n], 0, sems.at[n]))
+    for group in copies:
+        for c in group:
+            c.start()
     left = []
     dp = dp_ref[...]
     for n, (k, dy) in enumerate(order):
-        copies[n].wait()
+        for c in copies[n]:
+            c.wait()
         out = dot(dp, ws[n], NT).astype(BF)
         ps[dy, :, k * PW : (k + 1) * PW] = out[:, :PW]
         qs[k, :, dy * QW : (dy + 1) * QW] = out[:, PW:]
@@ -223,11 +220,6 @@
     xp, xq = x_own[:, :PW], x_own[:, PW:]
     got_p = [shift(xp, "x", k, 4) for k in (1, 2, 3)]
     got_q = swap(xq, "yl", 1, 2)
-    p_here = jnp.concatenate([xp] + got_p, axis=1)
-    q_here = jnp.concatenate([xq, got_q], axis=1)
-    p_there = swap(p_here, "yl", 1, 2)
-    q_there = [shift(q_here, "x", k, 4) for k in (1, 2, 3)]
-
     scaled = (x_own.astype(F32) * gain_own).astype(BF).T.reshape(2, 2, 160, TOK)
     to_core = lax.dynamic_index_in_dim(scaled, 1 - core, 1, False)
     mine = lax.dynamic_index_in_dim(scaled, core, 1, False)
@@ -235,9 +227,15 @@
     kept = lax.dynamic_index_in_dim(pair, yh, 0, False)
     got = swap(lax.dynamic_index_in_dim(pair, 1 - yh, 0, False), "yh", 1, 2)
     quarter = jnp.concatenate([kept, got], axis=1).reshape(160, 4 * TOK)
+    quarter, got_p, got_q = lax.optimization_barrier((quarter, got_p, got_q))
     group_x = lax.all_gather(quarter, ("yl", "x"), axis=0, tiled=True)
 
-    weight = w_qkv.reshape(8, SHARE, COLS)
+    p_here = jnp.concatenate([xp] + got_p, axis=1)
+    q_here = jnp.concatenate([xq, got_q], axis=1)
+    p_there = swap(p_here, "yl", 1, 2)
+    q_there = [shift(q_here, "x", k, 4) for k in (1, 2, 3)]
+
+    weight = w_qkv.transpose(1, 0, 2)
     gains = gain.reshape(8, 1, SHARE)
     gain_p, gain_q = gains[:, :, :PW], gains[:, :, PW:]
     acc, squares = pl.pallas_call(
@@ -251,7 +249,7 @@
         scratch_shapes=[
             pltpu.VMEM((4 * PW, COLS), BF),
             pltpu.VMEM((2 * QW, COLS), BF),
-            pltpu.SemaphoreType.DMA((6,)),
+            pltpu.SemaphoreType.DMA((6, 3)),
         ],
         compiler_params=PARAMS,
         cost_estimate=cost(2 * TOK * 1792 * COLS, 8_000_000),
@@ -277,7 +275,7 @@
             pltpu.VMEM((TOK, COLS), F32),
             pltpu.VMEM((4 * PW, COLS), BF),
             pltpu.VMEM((3, 2 * QW, COLS), BF),
-            pltpu.SemaphoreType.DMA((10,)),
+            pltpu.SemaphoreType.DMA((10, 3)),
         ],
         compiler_params=PARAMS,
         cost_estimate=cost(2 * TOK * 3328 * COLS + 4_000_000_000, 14_000_000),
@@ -289,8 +287,6 @@
 
     from_yh = swap(d_packed, "yh", 1, 2)
     from_core = swap(d_packed, "core", 1, 2)
-    from_both = swap(from_yh, "core", 1, 2)
-
     wide, narrow = 2 * QW, 4 * PW
     pieces = pl.pallas_call(
         feature_gradient,
@@ -302,7 +298,7 @@
         out_specs=(ANY,) * 6,
         scratch_shapes=[
             pltpu.VMEM((8, SHARE, COLS), BF),
-            pltpu.SemaphoreType.DMA((8,)),
+            pltpu.SemaphoreType.DMA((8, 3)),
             pltpu.VMEM((4, TOK, wide), BF),
             pltpu.VMEM((2, TOK, narrow), BF),
             pltpu.SemaphoreType.DMA((6,)),
@@ -312,26 +308,11 @@
         name="feature_gradient",
     )(targets, d_packed, weight)
     along_x = [shift(pieces[k], "x", k, 4) for k in (1, 2, 3)]
-    along_y = swap(pieces[5], "yl", 1, 2)
-    row_dots = lax.all_gather(stats[:, 0], ("yl", "x"), axis=0)
-    sum_q = sum((a.astype(F32) for a in along_x), pieces[0].astype(F32))
-    sum_p = pieces[4].astype(F32) + along_y.astype(F32)
-    sent_q = swap(sum_q[:, QW:].astype(BF), "yl", 1, 2)
-    sent_p = [
-        shift(sum_p[:, k * PW : (k + 1) * PW].astype(BF), "x", k, 4) for k in (1, 2, 3)
-    ]
-    own_q = sum_q[:, :QW] + sent_q.astype(F32)
-    own_p = sum((a.astype(F32) for a in sent_p), sum_p[:, :PW])
-    d_normed = jnp.concatenate([own_p, own_q], axis=1)
-    features = x_own.astype(F32)
-    row_dot = jnp.sum(row_dots, axis=0) * stats[:, 1]
-    input_gradient = (d_normed * gain_own - features * row_dot[:, None]).astype(BF)
-    gain_gradient = jnp.sum(d_normed * features, axis=0).reshape(5, 128)
-    for axis, bit, size in (
-        ("core", 1, 2), ("yh", 1, 2), ("z", 1, 8), ("z", 2, 8), ("z", 4, 8),
-    ):
-        gain_gradient = gain_gradient + swap(gain_gradient, axis, bit, size)
-
+
+    from_yh, from_core, along_x[0], along_x[2] = lax.optimization_barrier(
+        (from_yh, from_core, along_x[0], along_x[2])
+    )
+    from_both = swap(from_yh, "core", 1, 2)
     partial_weight = pl.pallas_call(
         weight_gradient,
         grid=(4,),
@@ -344,6 +325,28 @@
         name="weight_gradient",
     )(group_x, d_packed, from_core, from_yh, from_both)
     d_weight = lax.psum_scatter(partial_weight, "z", scatter_dimension=0, tiled=True)
+    along_y = swap(pieces[5], "yl", 1, 2)
+    row_dot = stats[:, 0]
+    for axis, bit, size in (("x", 1, 4), ("x", 2, 4), ("yl", 1, 2)):
+        row_dot = row_dot + swap(row_dot, axis, bit, size)
+    sum_q = sum((a.astype(F32) for a in along_x), pieces[0].astype(F32))
+    sum_p = pieces[4].astype(F32) + along_y.astype(F32)
+    sent_q = swap(sum_q[:, QW:].astype(BF), "yl", 1, 2)
+    sent_p = [
+        shift(sum_p[:, k * PW : (k + 1) * PW].astype(BF), "x", k, 4) for k in (1, 2, 3)
+    ]
+    own_q = sum_q[:, :QW] + sent_q.astype(F32)
+    own_p = sum((a.astype(F32) for a in sent_p), sum_p[:, :PW])
+    d_normed = jnp.concatenate([own_p, own_q], axis=1)
+    features = x_own.astype(F32)
+    row_dot = row_dot * stats[:, 1]
+    input_gradient = (d_normed * gain_own - features * row_dot[:, None]).astype(BF)
+    gain_gradient = jnp.sum(d_normed * features, axis=0).reshape(5, 128)
+    for axis, bit, size in (
+        ("core", 1, 2), ("yh", 1, 2), ("z", 1, 8), ("z", 2, 8), ("z", 4, 8),
+    ):
+        gain_gradient = gain_gradient + swap(gain_gradient, axis, bit, size)
+
     return (
         input_gradient,
         gain_gradient.reshape(SHARE),

time: 298 us -> 187 us (0.63)
  local copies, waits for them, and re-layouts: 58.5 us -> 12.1 us
  blocking collectives: 41.4 us -> 0 us
  waiting for transfers between devices: 101 us -> 71.2 us
  starting transfers between devices: 43.3 us -> 52.4 us
    reshape x2 -> x0, local copies, waits for them, and re-layouts: 48 us -> none  [body(): weight = w_qkv.reshape(8, SHARE, COLS)]
    ppermute x12, waiting for transfers between devices: 7.79 us -> 50.5 us  [shift(): lax.ppermute(values, axis, [(i, (i + by) % size) for i in range(size)])]
    unnamed x1 -> x0, blocking collectives: 41.4 us -> none
    reduce_scatter x1, waiting for transfers between devices: 29.2 us -> 0.01 us  [body(): lax.psum_scatter(partial_weight, 'z', scatter_dimension=0, tiled=True)]
    all_gather x1, waiting for transfers between devices: 28.2 us -> 0.01 us  [body(): group_x = lax.all_gather(quarter, ('yl', 'x'), axis=0, tiled=True)]
    ppermute x14 -> x17, waiting for transfers between devices: 35.5 us -> 20.6 us  [swap(): return lax.ppermute(values, axis, [(i, i ^ bit) for i in range(size)])]
    ppermute x14 -> x17, starting transfers between devices: 24 us -> 31.3 us  [swap(): return lax.ppermute(values, axis, [(i, i ^ bit) for i in range(size)])]
    unnamed x19 -> x32, local copies, waits for them, and re-layouts: 4.62 us -> 7.34 us
  transfers between devices with their start and end apart: 28 -> 31, of which waited for: 16 -> 23; matrix products, arithmetic and copies ran while one was open for 19% -> 3% of each run, Pallas kernels for 1% -> 13%
where the time goes in v2:
time: 187 us
  waiting for transfers between devices  71.2 us (38%)
  starting transfers between devices  52.4 us (28%)
  Pallas kernels  32.3 us (17%)
  between operations  14.4 us (8%)
  local copies, waits for them, and re-layouts  12.1 us (6%)
  other arithmetic  4.61 us (2%)
    ppermute x12, waiting for transfers between devices, shift(): lax.ppermute(values, axis, [(i, (i + by) % size) for i in range(size)])  50.5 us
    ppermute x17, starting transfers between devices, swap(): return lax.ppermute(values, axis, [(i, i ^ bit) for i in range(size)])  31.3 us
    ppermute x12, starting transfers between devices, shift(): lax.ppermute(values, axis, [(i, (i + by) % size) for i in range(size)])  21 us
    ppermute x17, waiting for transfers between devices, swap(): return lax.ppermute(values, axis, [(i, i ^ bit) for i in range(size)])  20.6 us
    pallas_call x1, Pallas kernels, body(): pl.pallas_call(feature_gradient, out_shape=tuple([jax.ShapeDtypeStruct((T...  11.5 us
    pallas_call x1, Pallas kernels, body(): pl.pallas_call(attention, out_shape=(jax.ShapeDtypeStruct((TOK, COLS), BF...  9.32 us
    unnamed x32, local copies, waits for them, and re-layouts  7.34 us
    pallas_call x1, Pallas kernels, body(): pl.pallas_call(weight_gradient, grid=(4,), out_shape=jax.ShapeDtypeStruct...  7.12 us
  transfers between devices with their start and end apart: 31, of which 23 were waited for; matrix products, arithmetic and copies ran while one was open for 3% of the time, Pallas kernels for 13%

profile of v2, /device:TPU:2, one launch (start us, length us, event | category | flops | bytes accessed | tf_op | source)
XLA Modules:
  0.0 187.0 jit_solution(615589330594239015)
XLA Ops:
  7.2 0.8 dynamic_slice.17
  8.0 1.1 fusion.4
  9.5 1.5 collective-permute-done
  11.1 3.3 %collective-permute-start.1 = (bf16[160,2,320]{2,0,1:T(8,128)(2,1)S(1)}, bf16[160,2,320]{2,0,1:T(8,128)(2,1)S(1)}, u32[]{:S(2)}, u32[]{:S(2)}) collective-permute-start(bf16[160,2,320]{2,0,1:T(8,128)(2,1)S(1)} %get-tuple-element.60), channel_id=1, source_target_pairs={{0,16},{16,0},{1,17},{17,1},{2,18},{18,2},{3,19},{19,3},{4,20},{20... | collective-permute-start | bytes 614408 | tf_op jit(solution)/shard_map/ppermute | solution.py:208
  14.5 0.8 collective-permute-start.5
  15.2 1.6 collective-permute-start.2
  16.8 1.1 collective-permute-start.3
  17.9 2.1 %collective-permute-start.4 = (bf16[320,256]{1,0:T(8,128)(2,1)S(1)}, bf16[320,256]{1,0:T(8,128)(2,1)S(1)}, u32[]{:S(2)}, u32[]{:S(2)}) collective-permute-start(bf16[320,256]{1,0:T(8,128)(2,1)S(1)} %slice.40), channel_id=1, source_target_pairs={{0,3},{1,0},{2,1},{3,2},{4,7},{5,4},{6,5},{7,6},{8,11},{9,8},{10,9... | collective-permute-start | bytes 491528 | tf_op jit(solution)/shard_map/ppermute | solution.py:204
  20.1 1.5 collective-permute-done.1
  21.9 1.2 reshape.35
  23.0 2.4 %collective-permute-done.3 = bf16[320,256]{1,0:T(8,128)(2,1)S(1)} collective-permute-done((bf16[320,256]{1,0:T(8,128)(2,1)S(1)}, bf16[320,256]{1,0:T(8,128)(2,1)S(1)}, u32[]{:S(2)}, u32[]{:S(2)}) %collective-permute-start.3) | collective-permute-done | bytes 163872 | tf_op jit(solution)/shard_map/ppermute | solution.py:204
  25.4 1.1 collective-permute-done.4
  26.8 1.4 collective-permute-start.6
  28.3 1.4 collective-permute-start.7
  29.7 1.5 collective-permute-start.8
  31.2 1.8 collective-permute-start.9
  33.2 0.6 fusion.13
  34.0 4.4 %project_first.1 = (f32[320,1152]{1,0:T(8,128)S(1)}, f32[320,128]{1,0:T(8,128)S(1)}) custom-call(s32[8]{0:T(128)S(1)} %pad_add_fusion.1.place_ref, bf16[320,1024]{1,0:T(8,128)(2,1)S(1)} %pad_maximum_fusion.1.p_ref, bf16[320,768]{1,0:T(8,128)(2,1)S(1)} %pad_maximum_fusion.3.q_ref, f32[8,1,256]{2,1,0:T(1,128)S(1)} %slice.52.gp_ref, ...), custom_call_target="tpu_custom_call" | custom-call | flops 1321205760 | bytes 8000000 | tf_op jit(solution)/shard_map/project_first/pallas_call | solution.py:241
  38.3 6.5 %collective-permute-done.7.q1_ref = bf16[320,768]{1,0:T(8,128)(2,1)S(1)} collective-permute-done((bf16[320,768]{1,0:T(8,128)(2,1)S(1)}, bf16[320,768]{1,0:T(8,128)(2,1)S(1)}, u32[]{:S(2)}, u32[]{:S(2)}) %collective-permute-start.7) | collective-permute-done | bytes 491552 | tf_op jit(solution)/shard_map/ppermute | solution.py:204
  44.8 4.0 %collective-permute-done.8.q2_ref = bf16[320,768]{1,0:T(8,128)(2,1)S(1)} collective-permute-done((bf16[320,768]{1,0:T(8,128)(2,1)S(1)}, bf16[320,768]{1,0:T(8,128)(2,1)S(1)}, u32[]{:S(2)}, u32[]{:S(2)}) %collective-permute-start.8) | collective-permute-done | bytes 491552 | tf_op jit(solution)/shard_map/ppermute | solution.py:204
  48.8 16.0 %collective-permute-done.9.q3_ref = bf16[320,768]{1,0:T(8,128)(2,1)S(1)} collective-permute-done((bf16[320,768]{1,0:T(8,128)(2,1)S(1)}, bf16[320,768]{1,0:T(8,128)(2,1)S(1)}, u32[]{:S(2)}, u32[]{:S(2)}) %collective-permute-start.9) | collective-permute-done | bytes 491552 | tf_op jit(solution)/shard_map/ppermute | solution.py:204
  64.8 9.3 %attention.1 = (bf16[320,1152]{1,0:T(8,128)(2,1)S(1)}, f32[320,128]{1,0:T(8,128)S(1)}) custom-call(s32[8]{0:T(128)S(1)} %pad_add_fusion.1.place_ref, f32[320,1152]{1,0:T(8,128)S(1)} %get-tuple-element.26.acc0_ref, f32[320,128]{1,0:T(8,128)S(1)} %get-tuple-element.27.sq0_ref, bf16[320,1024]{1,0:T(8,128)(2,1)S(1)} %collective-permute-done.6.p_ref, ...), custom_call_target="tpu_custom_call" | custom-call | flops 6453667840 | bytes 14000000 | tf_op jit(solution)/shard_map/attention/pallas_call | solution.py:266
  74.2 1.2 collective-permute-start.14
  75.3 11.5 %feature_gradient.1 = (bf16[320,768]{1,0:T(8,128)(2,1)S(1)}, bf16[320,768]{1,0:T(8,128)(2,1)S(1)}, bf16[320,768]{1,0:T(8,128)(2,1)S(1)}, bf16[320,768]{1,0:T(8,1...) custom-call(s32[8]{0:T(128)S(1)} %pad_add_fusion.place_ref, ...), custom_call_target="tpu_custom_call" | custom-call | flops 3774873600 | bytes 16000000 | tf_op jit(solution)/shard_map/feature_gradient/pallas_call | solution.py:291
  86.9 0.8 copy-done.3
  87.7 0.8 copy-done.5
  88.5 2.5 %collective-permute-start.16 = (bf16[320,768]{1,0:T(8,128)(2,1)S(1)}, bf16[320,768]{1,0:T(8,128)(2,1)S(1)}, u32[]{:S(2)}, u32[]{:S(2)}) collective-permute-start(bf16[320,768]{1,0:T(8,128)(2,1)S(1)} %get-tuple-element.32), channel_id=1, source_target_pairs={{0,1},{1,2},{2,3},{3,0},{4,5},{5,6},{6,7},{7,4},{8,9},{9,10},{10,1... | collective-permute-start | bytes 1474568 | tf_op jit(solution)/shard_map/ppermute | solution.py:204
  91.0 11.9 %collective-permute-done.16 = bf16[320,768]{1,0:T(8,128)(2,1)S(1)} collective-permute-done((bf16[320,768]{1,0:T(8,128)(2,1)S(1)}, bf16[320,768]{1,0:T(8,128)(2,1)S(1)}, u32[]{:S(2)}, u32[]{:S(2)}) %collective-permute-start.16) | collective-permute-done | bytes 491552 | tf_op jit(solution)/shard_map/ppermute | solution.py:204
  102.9 1.5 collective-permute-done.17
  104.5 0.7 copy-done.12
  105.2 1.5 collective-permute-done.28.d3
  106.7 0.9 copy-done.1
  107.6 1.9 %copy-done = bf16[1280,1280]{1,0:T(8,128)(2,1)S(1)} copy-done((bf16[1280,1280]{1,0:T(8,128)(2,1)S(1)}, bf16[1280,1280]{1,0:T(8,128)(2,1)}, u32[]{:S(2)}) %copy-start) | copy-done | bytes 3276824
  109.5 1.1 copy-done.2
  110.6 7.1 %weight_gradient.1 = bf16[1280,1152]{1,0:T(8,128)(2,1)} custom-call(bf16[1280,1280]{1,0:T(8,128)(2,1)S(1)} %copy-done, bf16[320,1152]{1,0:T(8,128)(2,1)S(1)} %get-tuple-element.28.dp_ref.d0, bf16[320,1152]{1,0:T(8,128)(2,1)S(1)} %collective-permute-done.15.d1, bf16[320,1152]{1,0:T(8,128)(2,1)S(1)} %collective-permute-done.14.d2, bf16[320,1152]{1,0:T(8,128)(2,1)S(1)} %copy-done.2), custom_call_target="tpu_custom_call" | custom-call | flops 3774873600 | bytes 10000000 | tf_op jit(solution)/shard_map/weight_gradient/pallas_call | solution.py:316
  117.8 1.0 copy-done.4
  119.1 2.2 %collective-permute-start.20 = (f32[320]{0:T(512)S(1)}, f32[320]{0:T(512)S(1)}, u32[]{:S(2)}, u32[]{:S(2)}) collective-permute-start(f32[320]{0:T(512)S(1)} %get-tuple-element.50), channel_id=1, source_target_pairs={{0,1},{1,0},{2,3},{3,2},{4,5},{5,4},{6,7},{7,6},{8,9},{9,8},{10,11... | collective-permute-start | bytes 3848 | tf_op jit(solution)/shard_map/ppermute | solution.py:208
  121.3 1.6 collective-permute-done.20
  122.9 3.1 %collective-permute-start.21 = (f32[320]{0:T(512)S(1)}, f32[320]{0:T(512)S(1)}, u32[]{:S(2)}, u32[]{:S(2)}) collective-permute-start(f32[320]{0:T(512)S(1)} %add.138), channel_id=1, source_target_pairs={{0,2},{1,3},{2,0},{3,1},{4,6},{5,7},{6,4},{7,5},{8,10},{9,11},{10,... | collective-permute-start | bytes 3848 | tf_op jit(solution)/shard_map/ppermute | solution.py:208
  126.0 2.0 %collective-permute-done.21 = f32[320]{0:T(512)S(1)} collective-permute-done((f32[320]{0:T(512)S(1)}, f32[320]{0:T(512)S(1)}, u32[]{:S(2)}, u32[]{:S(2)}) %collective-permute-start.21) | collective-permute-done | bytes 1312 | tf_op jit(solution)/shard_map/ppermute | solution.py:208
  128.0 2.0 %collective-permute-start.22 = (f32[320]{0:T(512)S(1)}, f32[320]{0:T(512)S(1)}, u32[]{:S(2)}, u32[]{:S(2)}) collective-permute-start(f32[320]{0:T(512)S(1)} %add.139), channel_id=1, source_target_pairs={{0,4},{4,0},{1,5},{5,1},{2,6},{6,2},{3,7},{7,3},{8,12},{12,8},{9,1... | collective-permute-start | bytes 3848 | tf_op jit(solution)/shard_map/ppermute | solution.py:208
  130.0 3.1 %collective-permute-start.18 = (bf16[320,768]{1,0:T(8,128)(2,1)S(1)}, bf16[320,768]{1,0:T(8,128)(2,1)S(1)}, u32[]{:S(2)}, u32[]{:S(2)}) collective-permute-start(bf16[320,768]{1,0:T(8,128)(2,1)S(1)} %copy-done.6), channel_id=1, source_target_pairs={{0,2},{1,3},{2,0},{3,1},{4,6},{5,7},{6,4},{7,5},{8,10},{9,11},{10,... | collective-permute-start | bytes 1474568 | tf_op jit(solution)/shard_map/ppermute | solution.py:204
  133.1 2.5 %collective-permute-done.22 = f32[320]{0:T(512)S(1)} collective-permute-done((f32[320]{0:T(512)S(1)}, f32[320]{0:T(512)S(1)}, u32[]{:S(2)}, u32[]{:S(2)}) %collective-permute-start.22) | collective-permute-done | bytes 1312 | tf_op jit(solution)/shard_map/ppermute | solution.py:208
  135.7 0.3 fusion.18
  136.0 2.2 %collective-permute-start.13 = (bf16[320,256]{1,0:T(8,128)(2,1)S(1)}, bf16[320,256]{1,0:T(8,128)(2,1)S(1)}, u32[]{:S(2)}, u32[]{:S(2)}) collective-permute-start(bf16[320,256]{1,0:T(8,128)(2,1)S(1)} %get-tuple-element.57), channel_id=1, source_target_pairs={{0,3},{1,0},{2,1},{3,2},{4,7},{5,4},{6,5},{7,6},{8,11},{9,8},{10,9... | collective-permute-start | bytes 491528 | tf_op jit(solution)/shard_map/ppermute | solution.py:204
  138.2 1.5 collective-permute-start.12
  139.7 2.3 %collective-permute-start.11 = (bf16[320,256]{1,0:T(8,128)(2,1)S(1)}, bf16[320,256]{1,0:T(8,128)(2,1)S(1)}, u32[]{:S(2)}, u32[]{:S(2)}) collective-permute-start(bf16[320,256]{1,0:T(8,128)(2,1)S(1)} %get-tuple-element.56), channel_id=1, source_target_pairs={{0,1},{1,2},{2,3},{3,0},{4,5},{5,6},{6,7},{7,4},{8,9},{9,10},{10,1... | collective-permute-start | bytes 491528 | tf_op jit(solution)/shard_map/ppermute | solution.py:204
  142.0 3.4 %collective-permute-done.18 = bf16[320,768]{1,0:T(8,128)(2,1)S(1)} collective-permute-done((bf16[320,768]{1,0:T(8,128)(2,1)S(1)}, bf16[320,768]{1,0:T(8,128)(2,1)S(1)}, u32[]{:S(2)}, u32[]{:S(2)}) %collective-permute-start.18) | collective-permute-done | bytes 491552 | tf_op jit(solution)/shard_map/ppermute | solution.py:204
  145.7 0.3 collective-permute-start.19
  146.0 1.7 collective-permute-done.13
  147.8 1.8 collective-permute-done.12
  149.8 2.2 %collective-permute-done.19 = bf16[320,384]{1,0:T(8,128)(2,1)S(1)} collective-permute-done((bf16[320,384]{1,0:T(8,128)(2,1)S(1)}, bf16[320,384]{1,0:T(8,128)(2,1)S(1)}, u32[]{:S(2)}, u32[]{:S(2)}) %collective-permute-start.19) | collective-permute-done | bytes 245792 | tf_op jit(solution)/shard_map/ppermute | solution.py:208
  152.1 1.0 fusion.3
  153.1 1.2 collective-permute-done.23
  154.2 3.1 %collective-permute-start.24 = (f32[5,128]{1,0:T(8,128)S(1)}, f32[5,128]{1,0:T(8,128)S(1)}, u32[]{:S(2)}, u32[]{:S(2)}) collective-permute-start(f32[5,128]{1,0:T(8,128)S(1)} %bitcast_add_fusion), channel_id=1, source_target_pairs={{0,16},{16,0},{1,17},{17,1},{2,18},{18,2},{3,19},{19,3},{4,20},{20... | collective-permute-start | bytes 7688 | tf_op jit(solution)/shard_map/ppermute | solution.py:208
  157.4 2.0 %collective-permute-done.24 = f32[5,128]{1,0:T(8,128)S(1)} collective-permute-done((f32[5,128]{1,0:T(8,128)S(1)}, f32[5,128]{1,0:T(8,128)S(1)}, u32[]{:S(2)}, u32[]{:S(2)}) %collective-permute-start.24) | collective-permute-done | bytes 2592 | tf_op jit(solution)/shard_map/ppermute | solution.py:208
  159.3 2.3 %collective-permute-start.25 = (f32[5,128]{1,0:T(8,128)S(1)}, f32[5,128]{1,0:T(8,128)S(1)}, u32[]{:S(2)}, u32[]{:S(2)}) collective-permute-start(f32[5,128]{1,0:T(8,128)S(1)} %fusion.20), channel_id=1, source_target_pairs={{0,32},{32,0},{64,96},{96,64},{128,160},{160,128},{192,224},{224,1... | collective-permute-start | bytes 7688 | tf_op jit(solution)/shard_map/ppermute | solution.py:208
  161.6 1.6 collective-permute-done.25
  163.2 4.1 %collective-permute-start.26 = (f32[5,128]{1,0:T(8,128)S(1)}, f32[5,128]{1,0:T(8,128)S(1)}, u32[]{:S(2)}, u32[]{:S(2)}) collective-permute-start(f32[5,128]{1,0:T(8,128)S(1)} %add.143), channel_id=1, source_target_pairs={{0,64},{32,96},{64,0},{96,32},{128,192},{160,224},{192,128},{224,1... | collective-permute-start | bytes 7688 | tf_op jit(solution)/shard_map/ppermute | solution.py:208
  167.3 1.6 collective-permute-done.26
  168.9 7.3 %collective-permute-start.27 = (f32[5,128]{1,0:T(8,128)S(1)}, f32[5,128]{1,0:T(8,128)S(1)}, u32[]{:S(2)}, u32[]{:S(2)}) collective-permute-start(f32[5,128]{1,0:T(8,128)S(1)} %add.144), channel_id=1, source_target_pairs={{0,128},{32,160},{64,192},{96,224},{128,0},{160,32},{192,64},{224,... | collective-permute-start | bytes 7688 | tf_op jit(solution)/shard_map/ppermute | solution.py:208
  176.2 1.6 collective-permute-done.27
  177.8 0.6 add_bitcast_fusion
  178.4 1.8 copy.18
  (76 shorter events, 2.7 us)
Async XLA Ops:
  7.2 100.4 %all-gather.2.cloned.1.call-start = ((), (), s32[]{:S(2)}) async-start(), calls=%async_computation.1 | async-start | bytes 3686400 | tf_op jit(solution)/shard_map/all_gather | solution.py:231
  9.1 5.4 %copy-start.8 = (bf16[320,640]{1,0:T(8,128)(2,1)S(1)}, bf16[320,640]{1,0:T(8,128)(2,1)}, u32[]{:S(2)}) copy-start(bf16[320,640]{1,0:T(8,128)(2,1)} %param.5) | copy-start | bytes 1228804
  9.4 1.6 collective-permute-start
  11.1 10.4 %collective-permute-start.1 = (bf16[160,2,320]{2,0,1:T(8,128)(2,1)S(1)}, bf16[160,2,320]{2,0,1:T(8,128)(2,1)S(1)}, u32[]{:S(2)}, u32[]{:S(2)}) collective-permute-start(bf16[160,2,320]{2,0,1:T(8,128)(2,1)S(1)} %get-tuple-element.60), channel_id=1, source_target_pairs={{0,16},{16,0},{1,17},{17,1},{2,18},{18,2},{3,19},{19,3},{4,20},{20... | collective-permute-start | bytes 614408 | tf_op jit(solution)/shard_map/ppermute | solution.py:208
  14.5 12.1 %collective-permute-start.5 = (bf16[320,384]{1,0:T(8,128)(2,1)S(1)}, bf16[320,384]{1,0:T(8,128)(2,1)S(1)}, u32[]{:S(2)}, u32[]{:S(2)}) collective-permute-start(bf16[320,384]{1,0:T(8,128)(2,1)S(1)} %slice.41), channel_id=1, source_target_pairs={{0,4},{4,0},{1,5},{5,1},{2,6},{6,2},{3,7},{7,3},{8,12},{12,8},{9,1... | collective-permute-start | bytes 737288 | tf_op jit(solution)/shard_map/ppermute | solution.py:208
  15.2 7.8 %collective-permute-start.2 = (bf16[320,256]{1,0:T(8,128)(2,1)S(1)}, bf16[320,256]{1,0:T(8,128)(2,1)S(1)}, u32[]{:S(2)}, u32[]{:S(2)}) collective-permute-start(bf16[320,256]{1,0:T(8,128)(2,1)S(1)} %slice.40), channel_id=1, source_target_pairs={{0,1},{1,2},{2,3},{3,0},{4,5},{5,6},{6,7},{7,4},{8,9},{9,10},{10,1... | collective-permute-start | bytes 491528 | tf_op jit(solution)/shard_map/ppermute | solution.py:204
  16.8 8.6 %collective-permute-start.3 = (bf16[320,256]{1,0:T(8,128)(2,1)S(1)}, bf16[320,256]{1,0:T(8,128)(2,1)S(1)}, u32[]{:S(2)}, u32[]{:S(2)}) collective-permute-start(bf16[320,256]{1,0:T(8,128)(2,1)S(1)} %slice.40), channel_id=1, source_target_pairs={{0,2},{1,3},{2,0},{3,1},{4,6},{5,7},{6,4},{7,5},{8,10},{9,11},{10,... | collective-permute-start | bytes 491528 | tf_op jit(solution)/shard_map/ppermute | solution.py:204
  17.9 8.6 %collective-permute-start.4 = (bf16[320,256]{1,0:T(8,128)(2,1)S(1)}, bf16[320,256]{1,0:T(8,128)(2,1)S(1)}, u32[]{:S(2)}, u32[]{:S(2)}) collective-permute-start(bf16[320,256]{1,0:T(8,128)(2,1)S(1)} %slice.40), channel_id=1, source_target_pairs={{0,3},{1,0},{2,1},{3,2},{4,7},{5,4},{6,5},{7,6},{8,11},{9,8},{10,9... | collective-permute-start | bytes 491528 | tf_op jit(solution)/shard_map/ppermute | solution.py:204
  23.0 10.0 %copy-start.14 = (f32[5120]{0:T(1024)S(1)}, f32[5120]{0:T(1024)}, u32[]{:S(2)}) copy-start(f32[5120]{0:T(1024)} %param.6) | copy-start | bytes 61444
  23.0 10.0 %copy-start.15 = (s32[320]{0:T(512)S(1)}, s32[320]{0:T(512)}, u32[]{:S(2)}) copy-start(s32[320]{0:T(512)} %param.8) | copy-start | bytes 3844
  26.6 151.8 %reduce-scatter.2.cloned.1.call-start = ((), (), s32[]{:S(2)}) async-start(), calls=%async_computation.2 | async-start | bytes 3317760 | tf_op jit(solution)/shard_map/reduce_scatter | solution.py:327
  26.8 38.0 %collective-permute-start.6 = (bf16[320,1024]{1,0:T(8,128)(2,1)S(1)}, bf16[320,1024]{1,0:T(8,128)(2,1)S(1)}, u32[]{:S(2)}, u32[]{:S(2)}) collective-permute-start(bf16[320,1024]{1,0:T(8,128)(2,1)S(1)} %pad_maximum_fusion.1.p_ref), channel_id=1, source_target_pairs={{0,4},{4,0},{1,5},{5,1},{2,6},{6,2},{3,7},{7,3},{8,12},{12,8},{9,1... | collective-permute-start | bytes 1966088 | tf_op jit(solution)/shard_map/ppermute | solution.py:208
  28.3 16.5 %collective-permute-start.7 = (bf16[320,768]{1,0:T(8,128)(2,1)S(1)}, bf16[320,768]{1,0:T(8,128)(2,1)S(1)}, u32[]{:S(2)}, u32[]{:S(2)}) collective-permute-start(bf16[320,768]{1,0:T(8,128)(2,1)S(1)} %pad_maximum_fusion.3.q_ref), channel_id=1, source_target_pairs={{0,1},{1,2},{2,3},{3,0},{4,5},{5,6},{6,7},{7,4},{8,9},{9,10},{10,1... | collective-permute-start | bytes 1474568 | tf_op jit(solution)/shard_map/ppermute | solution.py:204
  29.7 19.1 %collective-permute-start.8 = (bf16[320,768]{1,0:T(8,128)(2,1)S(1)}, bf16[320,768]{1,0:T(8,128)(2,1)S(1)}, u32[]{:S(2)}, u32[]{:S(2)}) collective-permute-start(bf16[320,768]{1,0:T(8,128)(2,1)S(1)} %pad_maximum_fusion.3.q_ref), channel_id=1, source_target_pairs={{0,2},{1,3},{2,0},{3,1},{4,6},{5,7},{6,4},{7,5},{8,10},{9,11},{10,... | collective-permute-start | bytes 1474568 | tf_op jit(solution)/shard_map/ppermute | solution.py:204
  31.2 33.7 %collective-permute-start.9 = (bf16[320,768]{1,0:T(8,128)(2,1)S(1)}, bf16[320,768]{1,0:T(8,128)(2,1)S(1)}, u32[]{:S(2)}, u32[]{:S(2)}) collective-permute-start(bf16[320,768]{1,0:T(8,128)(2,1)S(1)} %pad_maximum_fusion.3.q_ref), channel_id=1, source_target_pairs={{0,3},{1,0},{2,1},{3,2},{4,7},{5,4},{6,5},{7,6},{8,11},{9,8},{10,9... | collective-permute-start | bytes 1474568 | tf_op jit(solution)/shard_map/ppermute | solution.py:204
  33.9 30.9 %copy-start.7 = (bf16[320,384]{1,0:T(8,128)(2,1)S(1)}, bf16[320,384]{1,0:T(8,128)(2,1)}, u32[]{:S(2)}) copy-start(bf16[320,384]{1,0:T(8,128)(2,1)} %dctx_ref.1) | copy-start | bytes 737284
  74.2 30.2 %collective-permute-start.14 = (bf16[320,1152]{1,0:T(8,128)(2,1)S(1)}, bf16[320,1152]{1,0:T(8,128)(2,1)S(1)}, u32[]{:S(2)}, u32[]{:S(2)}) collective-permute-start(bf16[320,1152]{1,0:T(8,128)(2,1)S(1)} %get-tuple-element.28.dp_ref.d0), channel_id=1, source_target_pairs={{0,16},{16,0},{1,17},{17,1},{2,18},{18,2},{3,19},{19,3},{4,20},{20... | collective-permute-start | bytes 2211848 | tf_op jit(solution)/shard_map/ppermute | solution.py:208
  75.3 29.1 %collective-permute-start.15 = (bf16[320,1152]{1,0:T(8,128)(2,1)S(1)}, bf16[320,1152]{1,0:T(8,128)(2,1)S(1)}, u32[]{:S(2)}, u32[]{:S(2)}) collective-permute-start(bf16[320,1152]{1,0:T(8,128)(2,1)S(1)} %get-tuple-element.28.dp_ref.d0), channel_id=1, source_target_pairs={{0,8},{8,0},{1,9},{9,1},{2,10},{10,2},{3,11},{11,3},{4,12},{12,4},... | collective-permute-start | bytes 2211848 | tf_op jit(solution)/shard_map/ppermute | solution.py:208
  86.9 0.9 copy-start.3
  87.7 0.8 copy-start.5
  88.5 14.4 %collective-permute-start.16 = (bf16[320,768]{1,0:T(8,128)(2,1)S(1)}, bf16[320,768]{1,0:T(8,128)(2,1)S(1)}, u32[]{:S(2)}, u32[]{:S(2)}) collective-permute-start(bf16[320,768]{1,0:T(8,128)(2,1)S(1)} %get-tuple-element.32), channel_id=1, source_target_pairs={{0,1},{1,2},{2,3},{3,0},{4,5},{5,6},{6,7},{7,4},{8,9},{9,10},{10,1... | collective-permute-start | bytes 1474568 | tf_op jit(solution)/shard_map/ppermute | solution.py:204
  91.0 13.4 %collective-permute-start.17 = (bf16[320,768]{1,0:T(8,128)(2,1)S(1)}, bf16[320,768]{1,0:T(8,128)(2,1)S(1)}, u32[]{:S(2)}, u32[]{:S(2)}) collective-permute-start(bf16[320,768]{1,0:T(8,128)(2,1)S(1)} %get-tuple-element.33), channel_id=1, source_target_pairs={{0,3},{1,0},{2,1},{3,2},{4,7},{5,4},{6,5},{7,6},{8,11},{9,8},{10,9... | collective-permute-start | bytes 1474568 | tf_op jit(solution)/shard_map/ppermute | solution.py:204
  102.9 1.5 copy-start.10
  104.4 0.8 copy-start.12
  104.4 2.3 %collective-permute-start.28 = (bf16[320,1152]{1,0:T(8,128)(2,1)S(1)}, bf16[320,1152]{1,0:T(8,128)(2,1)S(1)}, u32[]{:S(2)}, u32[]{:S(2)}) collective-permute-start(bf16[320,1152]{1,0:T(8,128)(2,1)S(1)} %collective-permute-done.14.d2), channel_id=1, source_target_pairs={{0,8},{8,0},{1,9},{9,1},{2,10},{10,2},{3,11},{11,3},{4,12},{12,4},... | collective-permute-start | bytes 2211848 | tf_op jit(solution)/shard_map/ppermute | solution.py:208
  106.7 0.9 copy-start.1
  107.6 1.9 %copy-start = (bf16[1280,1280]{1,0:T(8,128)(2,1)S(1)}, bf16[1280,1280]{1,0:T(8,128)(2,1)}, u32[]{:S(2)}) copy-start(bf16[1280,1280]{1,0:T(8,128)(2,1)} %all-gather.2.cloned.1.call-done.x_ref) | copy-start | bytes 9830404
  109.5 1.1 copy-start.2
  117.8 1.1 copy-start.4
  117.8 12.2 %copy-start.6 = (bf16[320,768]{1,0:T(8,128)(2,1)S(1)}, bf16[320,768]{1,0:T(8,128)(2,1)}, u32[]{:S(2)}) copy-start(bf16[320,768]{1,0:T(8,128)(2,1)} %copy-done.5) | copy-start | bytes 1474564
  118.9 16.8 %collective-permute-start.10 = (bf16[320,1024]{1,0:T(8,128)(2,1)S(1)}, bf16[320,1024]{1,0:T(8,128)(2,1)S(1)}, u32[]{:S(2)}, u32[]{:S(2)}) collective-permute-start(bf16[320,1024]{1,0:T(8,128)(2,1)S(1)} %copy-done.4), channel_id=1, source_target_pairs={{0,4},{4,0},{1,5},{5,1},{2,6},{6,2},{3,7},{7,3},{8,12},{12,8},{9,1... | collective-permute-start | bytes 1966088 | tf_op jit(solution)/shard_map/ppermute | solution.py:208
  119.1 3.8 %collective-permute-start.20 = (f32[320]{0:T(512)S(1)}, f32[320]{0:T(512)S(1)}, u32[]{:S(2)}, u32[]{:S(2)}) collective-permute-start(f32[320]{0:T(512)S(1)} %get-tuple-element.50), channel_id=1, source_target_pairs={{0,1},{1,0},{2,3},{3,2},{4,5},{5,4},{6,7},{7,6},{8,9},{9,8},{10,11... | collective-permute-start | bytes 3848 | tf_op jit(solution)/shard_map/ppermute | solution.py:208
  122.9 5.1 %collective-permute-start.21 = (f32[320]{0:T(512)S(1)}, f32[320]{0:T(512)S(1)}, u32[]{:S(2)}, u32[]{:S(2)}) collective-permute-start(f32[320]{0:T(512)S(1)} %add.138), channel_id=1, source_target_pairs={{0,2},{1,3},{2,0},{3,1},{4,6},{5,7},{6,4},{7,5},{8,10},{9,11},{10,... | collective-permute-start | bytes 3848 | tf_op jit(solution)/shard_map/ppermute | solution.py:208
  128.0 7.7 %collective-permute-start.22 = (f32[320]{0:T(512)S(1)}, f32[320]{0:T(512)S(1)}, u32[]{:S(2)}, u32[]{:S(2)}) collective-permute-start(f32[320]{0:T(512)S(1)} %add.139), channel_id=1, source_target_pairs={{0,4},{4,0},{1,5},{5,1},{2,6},{6,2},{3,7},{7,3},{8,12},{12,8},{9,1... | collective-permute-start | bytes 3848 | tf_op jit(solution)/shard_map/ppermute | solution.py:208
  130.0 15.4 %collective-permute-start.18 = (bf16[320,768]{1,0:T(8,128)(2,1)S(1)}, bf16[320,768]{1,0:T(8,128)(2,1)S(1)}, u32[]{:S(2)}, u32[]{:S(2)}) collective-permute-start(bf16[320,768]{1,0:T(8,128)(2,1)S(1)} %copy-done.6), channel_id=1, source_target_pairs={{0,2},{1,3},{2,0},{3,1},{4,6},{5,7},{6,4},{7,5},{8,10},{9,11},{10,... | collective-permute-start | bytes 1474568 | tf_op jit(solution)/shard_map/ppermute | solution.py:204
  136.0 9.5 %copy-start.11 = (bf16[320,768]{1,0:T(8,128)(2,1)S(1)}, bf16[320,768]{1,0:T(8,128)(2,1)}, u32[]{:S(2)}) copy-start(bf16[320,768]{1,0:T(8,128)(2,1)} %copy-done.10) | copy-start | bytes 1474564
  136.0 9.4 %copy-start.13 = (bf16[320,768]{1,0:T(8,128)(2,1)S(1)}, bf16[320,768]{1,0:T(8,128)(2,1)}, u32[]{:S(2)}) copy-start(bf16[320,768]{1,0:T(8,128)(2,1)} %copy-done.12) | copy-start | bytes 1474564
  136.0 11.7 %collective-permute-start.13 = (bf16[320,256]{1,0:T(8,128)(2,1)S(1)}, bf16[320,256]{1,0:T(8,128)(2,1)S(1)}, u32[]{:S(2)}, u32[]{:S(2)}) collective-permute-start(bf16[320,256]{1,0:T(8,128)(2,1)S(1)} %get-tuple-element.57), channel_id=1, source_target_pairs={{0,3},{1,0},{2,1},{3,2},{4,7},{5,4},{6,5},{7,6},{8,11},{9,8},{10,9... | collective-permute-start | bytes 491528 | tf_op jit(solution)/shard_map/ppermute | solution.py:204
  138.2 11.3 %collective-permute-start.12 = (bf16[320,256]{1,0:T(8,128)(2,1)S(1)}, bf16[320,256]{1,0:T(8,128)(2,1)S(1)}, u32[]{:S(2)}, u32[]{:S(2)}) collective-permute-start(bf16[320,256]{1,0:T(8,128)(2,1)S(1)} %get-tuple-element.58), channel_id=1, source_target_pairs={{0,2},{1,3},{2,0},{3,1},{4,6},{5,7},{6,4},{7,5},{8,10},{9,11},{10,... | collective-permute-start | bytes 491528 | tf_op jit(solution)/shard_map/ppermute | solution.py:204
  139.7 10.1 %collective-permute-start.11 = (bf16[320,256]{1,0:T(8,128)(2,1)S(1)}, bf16[320,256]{1,0:T(8,128)(2,1)S(1)}, u32[]{:S(2)}, u32[]{:S(2)}) collective-permute-start(bf16[320,256]{1,0:T(8,128)(2,1)S(1)} %get-tuple-element.56), channel_id=1, source_target_pairs={{0,1},{1,2},{2,3},{3,0},{4,5},{5,6},{6,7},{7,4},{8,9},{9,10},{10,1... | collective-permute-start | bytes 491528 | tf_op jit(solution)/shard_map/ppermute | solution.py:204
  145.7 6.4 %copy-start.9 = (bf16[320,640]{1,0:T(8,128)(2,1)S(1)}, bf16[320,640]{1,0:T(8,128)(2,1)}, u32[]{:S(2)}) copy-start(bf16[320,640]{1,0:T(8,128)(2,1)} %param.5) | copy-start | bytes 1228804
  145.7 6.3 %collective-permute-start.19 = (bf16[320,384]{1,0:T(8,128)(2,1)S(1)}, bf16[320,384]{1,0:T(8,128)(2,1)S(1)}, u32[]{:S(2)}, u32[]{:S(2)}) collective-permute-start(bf16[320,384]{1,0:T(8,128)(2,1)S(1)} %slice.69), channel_id=1, source_target_pairs={{0,4},{4,0},{1,5},{5,1},{2,6},{6,2},{3,7},{7,3},{8,12},{12,8},{9,1... | collective-permute-start | bytes 737288 | tf_op jit(solution)/shard_map/ppermute | solution.py:208
  153.1 1.2 collective-permute-start.23
  154.2 5.1 %collective-permute-start.24 = (f32[5,128]{1,0:T(8,128)S(1)}, f32[5,128]{1,0:T(8,128)S(1)}, u32[]{:S(2)}, u32[]{:S(2)}) collective-permute-start(f32[5,128]{1,0:T(8,128)S(1)} %bitcast_add_fusion), channel_id=1, source_target_pairs={{0,16},{16,0},{1,17},{17,1},{2,18},{18,2},{3,19},{19,3},{4,20},{20... | collective-permute-start | bytes 7688 | tf_op jit(solution)/shard_map/ppermute | solution.py:208
  159.3 3.8 %collective-permute-start.25 = (f32[5,128]{1,0:T(8,128)S(1)}, f32[5,128]{1,0:T(8,128)S(1)}, u32[]{:S(2)}, u32[]{:S(2)}) collective-permute-start(f32[5,128]{1,0:T(8,128)S(1)} %fusion.20), channel_id=1, source_target_pairs={{0,32},{32,0},{64,96},{96,64},{128,160},{160,128},{192,224},{224,1... | collective-permute-start | bytes 7688 | tf_op jit(solution)/shard_map/ppermute | solution.py:208
  163.2 5.7 %collective-permute-start.26 = (f32[5,128]{1,0:T(8,128)S(1)}, f32[5,128]{1,0:T(8,128)S(1)}, u32[]{:S(2)}, u32[]{:S(2)}) collective-permute-start(f32[5,128]{1,0:T(8,128)S(1)} %add.143), channel_id=1, source_target_pairs={{0,64},{32,96},{64,0},{96,32},{128,192},{160,224},{192,128},{224,1... | collective-permute-start | bytes 7688 | tf_op jit(solution)/shard_map/ppermute | solution.py:208
  168.9 8.9 %collective-permute-start.27 = (f32[5,128]{1,0:T(8,128)S(1)}, f32[5,128]{1,0:T(8,128)S(1)}, u32[]{:S(2)}, u32[]{:S(2)}) collective-permute-start(f32[5,128]{1,0:T(8,128)S(1)} %add.144), channel_id=1, source_target_pairs={{0,128},{32,160},{64,192},{96,224},{128,0},{160,32},{192,64},{224,... | collective-permute-start | bytes 7688 | tf_op jit(solution)/shard_map/ppermute | solution.py:208
Sparse Core Ops, SparseCore 0:
  26.7 57.4 all-gather.1
  117.9 49.5 reduce-scatter.1
